TPU v7x, 32 devices: a whole 2x2x4 slice. The times are simulated.
32 devices in a mesh: tile: 16 (over z, y, core), seg: 2 (over x).
Axes of the slice: x: 2, y: 2, z: 4, core: 2. Of those that a mesh axis runs over, the one named last changes fastest.
Arguments:
- right_sides: float32 [65536, 512], P(('tile', 'seg')), may hold values from -6 to 6
- leaf_proj: float32 [16, 32, 64, 128], P('tile', 'seg'), may hold values from -0.5 to 0.5
- col_levels: float32 [16, 4, 16, 128, 128], P('tile', None, 'seg'), may hold values from -0.5 to 0.5
- middle_factor: float32 [16, 32, 64, 64], P('tile', 'seg'), may hold values from -0.75 to 0.75
- row_levels: float32 [16, 4, 16, 128, 128], P('tile', None, 'seg'), may hold values from -0.5 to 0.5
- leaf_expand: float32 [16, 32, 128, 64], P('tile', 'seg'), may hold values from -0.1875 to 0.1875
Outputs:
- product: float32 [4096, 512], P(('seg', 'tile'))
All inputs are finite; a program needn't handle non-finite values.
Results may differ from a plain program's by a relative error of at most 0.0001.
Values sent between devices are 32-bit elements; how exact they have to be, the bound alone decides.
No kernel may reach another device: no remote copies, remote signals or barrier semaphores. Data moves between devices by JAX's collectives and lax.ppermute only.
A program may use at most 64 MiB of HBM per device.

v0:
```python
import jax
import jax.numpy as jnp
from jax import lax
from jax.sharding import PartitionSpec as P

K = 64
LEAF = 128
LVL = 4
BOX = 16


def levels(coeffs, weights):
    width = coeffs.shape[-1]
    for level in range(LVL):
        stride = 2**level
        blocks = BOX // (2 * stride)
        wide = weights[level].reshape(blocks, stride, 2, K, 2, K)
        split = coeffs.reshape(blocks, 2, stride, K, width)
        mixed = jnp.einsum("aeuvwx,awexr->auevr", wide, split, precision=lax.Precision.HIGHEST)
        coeffs = mixed.reshape(BOX, K, width)
    return coeffs


def tile_product(columns, leaf_proj, col_levels, middle_factor, row_levels, leaf_expand):
    width = columns.shape[1]
    coeffs = jnp.einsum(
        "nkl,nlr->nkr",
        leaf_proj[0],
        columns.reshape(BOX, LEAF, width),
        precision=lax.Precision.HIGHEST,
    )
    coeffs = levels(coeffs, col_levels[0])
    coeffs = jnp.einsum("nkj,njr->nkr", middle_factor[0], coeffs, precision=lax.Precision.HIGHEST)
    coeffs = lax.all_to_all(coeffs, "seg", split_axis=0, concat_axis=0, tiled=True)
    coeffs = levels(coeffs, row_levels[0])
    expand = leaf_expand[0]
    out_rows = BOX * LEAF // lax.axis_size("tile")
    leaf_count = min(BOX, lax.axis_size("tile") * out_rows // LEAF + 2)
    rows = jnp.einsum("nlk,nkr->nlr", expand, coeffs, precision=lax.Precision.HIGHEST)
    rows = rows.reshape(leaf_count * LEAF, width)
    return lax.psum_scatter(rows, "tile", scatter_dimension=0, tiled=True)


def shards(right_sides, leaf_proj, col_levels, middle_factor, row_levels, leaf_expand):
    return tile_product(right_sides, leaf_proj, col_levels, middle_factor, row_levels, leaf_expand)


def solution(mesh):
    in_specs = (
        P(("tile", "seg"), None),
        P("tile", "seg", None, None),
        P("tile", None, "seg", None, None),
        P("tile", "seg", None, None),
        P("tile", None, "seg", None, None),
        P("tile", "seg", None, None),
    )
    out_specs = P(("seg", "tile"), None)
    return jax.shard_map(shards, mesh=mesh, in_specs=in_specs, out_specs=out_specs, check_vma=False)
```

profile of v0, /device:TPU:0, one launch (start us, length us, event | category | flops | bytes accessed | tf_op | source)
XLA Modules:
  0.0 163.2 jit_solution(6327818611411840116)
XLA Ops:
  6.5 0.0 copy-start
  6.5 2.7 %fusion.46 = (f32[1,1,8,128,128]{4,3,2,1,0:T(8,128)S(1)}, f32[1,1,8,128,128]{4,3,2,1,0:T(8,128)}, f32[1,1,8,128,128]{4,3,2,1,0:T(8,128)S(1)}, f32[1,1,8,128,128]{4,3,2,1,0:T(8,128)}) fusion(f32[1,4,8,128,128]{4,3,2,1,0:T(8,128)} %param.8), kind=kLoop, calls=%fused_computation.35 | loop fusion | bytes 4194304 | tf_op jit(solution)/shard_map/slice | solution.py:17
  9.3 0.6 reshape.68
  9.9 1.7 %reshape_squeeze.16 = f32[4,2,2,64,2,64]{5,4,3,2,1,0:T(2,128)S(1)} reshape(f32[1,1,8,128,128]{4,3,2,1,0:T(8,128)} %get-tuple-element.10) | data formatting | bytes 1048576 | tf_op jit(solution)/shard_map/reshape;squeeze | solution.py:17
  11.6 4.5 %fusion.43 = f32[16,64,512]{2,1,0:T(8,128)S(1)} fusion(f32[16,128,512]{2,1,0:T(8,128)} %bitcast.129, f32[1,16,64,128]{3,2,1,0:T(8,128)} %param.7), kind=kOutput, calls=%fused_computation.32 | convolution fusion | flops 805306368 | bytes 6815744 | tf_op jit(solution)/shard_map/nkl,nlr->nkr/dot_general | solution.py:26
  16.1 2.1 %fusion.38 = f32[8,512,2,64,1]{1,3,4,2,0:T(8,128)S(1)} fusion(f32[8,2,64,512,1]{3,2,1,4,0:T(8,128)S(1)} %bitcast.126, f32[8,2,64,2,64]{4,3,2,1,0:T(2,128)S(1)} %reshape.68), kind=kOutput, calls=%fused_computation.27 | convolution fusion | flops 805306368 | bytes 4718592 | tf_op jit(solution)/shard_map/aeuvwx,awexr->auevr/dot_general | solution.py:19
  18.2 2.1 %fusion.12 = f32[4,2,2,64,512]{4,3,1,2,0:T(8,128)S(1)} fusion(f32[4,2,2,64,512,1]{4,3,2,1,0,5:T(8,128)S(1)} %bitcast.121, f32[4,2,2,64,2,64]{5,4,3,2,1,0:T(2,128)S(1)} %reshape_squeeze.16), kind=kOutput, calls=%fused_computation.12 | convolution fusion | flops 805306368 | bytes 4718592 | tf_op jit(solution)/shard_map/aeuvwx,awexr->auevr/dot_general | solution.py:19
  20.2 0.2 copy.12
  20.4 2.6 %reshape_squeeze.17 = f32[2,4,2,64,2,64]{5,4,3,2,1,0:T(2,128)} reshape(f32[1,1,8,128,128]{4,3,2,1,0:T(8,128)} %get-tuple-element.12) | data formatting | bytes 1048576 | tf_op jit(solution)/shard_map/reshape;squeeze | solution.py:17
  23.0 3.2 %fusion.15 = f32[2,2,4,64,512]{4,3,1,2,0:T(8,128)S(1)} fusion(f32[2,2,4,64,512,1]{4,3,2,1,0,5:T(8,128)S(1)} %bitcast.122, f32[2,4,2,64,2,64]{5,4,3,2,1,0:T(2,128)} %reshape_squeeze.17), kind=kOutput, calls=%fused_computation.13 | convolution fusion | flops 805306368 | bytes 4718592 | tf_op jit(solution)/shard_map/aeuvwx,awexr->auevr/dot_general | solution.py:19
  26.3 0.2 copy.15
  26.5 1.6 reshape.70
  28.0 3.2 %fusion.18 = f32[1,2,8,64,512]{4,3,1,2,0:T(8,128)S(1)} fusion(f32[2,8,64,512,1]{3,2,1,0,4:T(8,128)S(1)} %bitcast.120, f32[8,2,64,2,64]{4,3,2,1,0:T(2,128)} %reshape.70), kind=kOutput, calls=%fused_computation.14 | convolution fusion | flops 805306368 | bytes 4718592 | tf_op jit(solution)/shard_map/aeuvwx,awexr->auevr/dot_general | solution.py:19
  31.3 0.0 copy-start.4
  31.3 0.2 copy.18
  31.5 0.8 copy-done.4
  32.3 3.5 %convolution_bitcast_fusion = f32[16,64,512]{2,1,0:T(8,128)} fusion(f32[16,64,512]{2,1,0:T(8,128)S(1)} %bitcast.127, f32[1,16,64,64]{3,2,1,0:T(8,128)S(1)} %copy-done.4), kind=kOutput, calls=%fused_computation.18 | convolution fusion | flops 402653184 | bytes 4456448 | tf_op jit(solution)/shard_map/nkj,njr->nkr/dot_general | solution.py:33
  35.9 4.2 %all-to-all-start = ((f32[16,64,512]{2,1,0:T(8,128)}), f32[16,64,512]{2,1,0:T(8,128)S(1)}, u32[]{:S(2)}, u32[]{:S(2)}) async-start(f32[16,64,512]{2,1,0:T(8,128)} %convolution_bitcast_fusion), calls=%async_computation | async-start | bytes 4194304 | tf_op jit(solution)/shard_map/all_to_all | solution.py:34
  40.1 0.0 reduce-scatter.2.cloned.1.call-start
  40.1 2.7 %fusion.45 = (f32[1,1,8,128,128]{4,3,2,1,0:T(8,128)S(1)}, f32[1,1,8,128,128]{4,3,2,1,0:T(8,128)}, f32[1,1,8,128,128]{4,3,2,1,0:T(8,128)}, f32[1,1,8,128,128]{4,3,2,1,0:T(8,128)}) fusion(f32[1,4,8,128,128]{4,3,2,1,0:T(8,128)} %param.10), kind=kLoop, calls=%fused_computation.34 | loop fusion | bytes 4194304 | tf_op jit(solution)/shard_map/slice | solution.py:17
  42.8 2.6 %reshape.73 = f32[8,2,64,2,64]{4,3,2,1,0:T(2,128)} reshape(f32[1,1,8,128,128]{4,3,2,1,0:T(8,128)} %get-tuple-element.7) | data formatting | bytes 1048576 | tf_op jit(solution)/shard_map/reshape.23
  45.4 2.6 %reshape_squeeze.18 = f32[4,2,2,64,2,64]{5,4,3,2,1,0:T(2,128)} reshape(f32[1,1,8,128,128]{4,3,2,1,0:T(8,128)} %get-tuple-element.6) | data formatting | bytes 1048576 | tf_op jit(solution)/shard_map/reshape;squeeze | solution.py:17
  48.1 2.6 %reshape_squeeze.19 = f32[2,4,2,64,2,64]{5,4,3,2,1,0:T(2,128)} reshape(f32[1,1,8,128,128]{4,3,2,1,0:T(8,128)} %get-tuple-element.8) | data formatting | bytes 1048576 | tf_op jit(solution)/shard_map/reshape;squeeze | solution.py:17
  50.7 1.6 reshape.75
  52.3 13.6 %all-to-all-done = f32[16,64,512]{2,1,0:T(8,128)S(1)} async-done(((f32[16,64,512]{2,1,0:T(8,128)}), f32[16,64,512]{2,1,0:T(8,128)S(1)}, u32[]{:S(2)}, u32[]{:S(2)}) %all-to-all-start) | async-done | bytes 2097184 | tf_op jit(solution)/shard_map/all_to_all | solution.py:34
  65.9 0.0 copy-start.3
  65.9 3.3 %fusion.33 = f32[8,512,2,64,1]{1,3,4,2,0:T(8,128)S(1)} fusion(f32[8,2,64,512,1]{3,2,1,4,0:T(8,128)S(1)} %bitcast.119, f32[8,2,64,2,64]{4,3,2,1,0:T(2,128)} %reshape.73), kind=kOutput, calls=%fused_computation.22 | convolution fusion | flops 805306368 | bytes 4718592 | tf_op jit(solution)/shard_map/aeuvwx,awexr->auevr/dot_general | solution.py:19
  69.3 0.0 copy-done.3
  69.3 2.0 %fusion.21 = f32[4,2,2,64,512]{4,3,1,2,0:T(8,128)S(1)} fusion(f32[4,2,2,64,512,1]{4,3,2,1,0,5:T(8,128)S(1)} %bitcast.123, f32[4,2,2,64,2,64]{5,4,3,2,1,0:T(2,128)S(1)} %copy-done.3), kind=kOutput, calls=%fused_computation.15 | convolution fusion | flops 805306368 | bytes 4718592 | tf_op jit(solution)/shard_map/aeuvwx,awexr->auevr/dot_general | solution.py:19
  71.3 0.0 copy-start.2
  71.3 0.2 copy.22
  71.6 1.0 copy-done.2
  72.6 2.0 %fusion.24 = f32[2,2,4,64,512]{4,3,1,2,0:T(8,128)S(1)} fusion(f32[2,2,4,64,512,1]{4,3,2,1,0,5:T(8,128)S(1)} %bitcast.124, f32[2,4,2,64,2,64]{5,4,3,2,1,0:T(2,128)S(1)} %copy-done.2), kind=kOutput, calls=%fused_computation.16 | convolution fusion | flops 805306368 | bytes 4718592 | tf_op jit(solution)/shard_map/aeuvwx,awexr->auevr/dot_general | solution.py:19
  74.6 0.0 copy-start.1
  74.6 0.2 copy.25
  74.8 1.0 copy-done.1
  75.8 2.0 %fusion.27 = f32[1,2,8,64,512]{4,3,1,2,0:T(8,128)S(1)} fusion(f32[2,8,64,512,1]{3,2,1,0,4:T(8,128)S(1)} %bitcast.125, f32[8,2,64,2,64]{4,3,2,1,0:T(2,128)S(1)} %copy-done.1), kind=kOutput, calls=%fused_computation.17 | convolution fusion | flops 805306368 | bytes 4718592 | tf_op jit(solution)/shard_map/aeuvwx,awexr->auevr/dot_general | solution.py:19
  77.9 0.2 copy.28
  78.1 0.0 copy-done
  78.1 5.1 %fusion.40 = f32[16,512,128]{1,2,0:T(8,128)} fusion(f32[16,64,512]{2,1,0:T(8,128)S(1)} %bitcast.128, f32[1,16,128,64]{2,3,1,0:T(8,128)S(1)} %copy-done), kind=kOutput, calls=%fused_computation.29 | convolution fusion | flops 805306368 | bytes 6815744 | tf_op jit(solution)/shard_map/nlk,nkr->nlr/dot_general | solution.py:39
  83.2 0.0 reduce-scatter.2.cloned.1.call-update
  83.2 73.2 %reduce-scatter.2.cloned.1.call-done = f32[128,512]{1,0:T(8,128)} async-done(((f32[2048,512]{1,0:T(8,128)}), f32[128,512]{1,0:T(8,128)}) %reduce-scatter.2.cloned.1.call-update) | async-done | bytes 262160 | tf_op jit(solution)/shard_map/reduce_scatter | solution.py:41
Async XLA Ops:
  6.5 71.6 %copy-start = (f32[1,16,128,64]{2,3,1,0:T(8,128)S(1)}, f32[1,16,128,64]{2,3,1,0:T(8,128)}, u32[]{:S(2)}) copy-start(f32[1,16,128,64]{2,3,1,0:T(8,128)} %param.11) | copy-start | bytes 1572868
  31.3 1.0 copy-start.4
  35.9 30.1 %all-to-all-start = ((f32[16,64,512]{2,1,0:T(8,128)}), f32[16,64,512]{2,1,0:T(8,128)S(1)}, u32[]{:S(2)}, u32[]{:S(2)}) async-start(f32[16,64,512]{2,1,0:T(8,128)} %convolution_bitcast_fusion), calls=%async_computation | async-start | bytes 4194304 | tf_op jit(solution)/shard_map/all_to_all | solution.py:34
  40.1 116.3 %reduce-scatter.2.cloned.1.call-start = ((), (), s32[]{:S(2)}) async-start(), calls=%async_computation.2 | async-start | bytes 4456448 | tf_op jit(solution)/shard_map/reduce_scatter | solution.py:41
  65.9 3.4 %copy-start.3 = (f32[4,2,2,64,2,64]{5,4,3,2,1,0:T(2,128)S(1)}, f32[4,2,2,64,2,64]{5,4,3,2,1,0:T(2,128)}, u32[]{:S(2)}) copy-start(f32[4,2,2,64,2,64]{5,4,3,2,1,0:T(2,128)} %reshape_squeeze.18) | copy-start | bytes 1572868
  71.3 1.2 copy-start.2
  74.6 1.2 copy-start.1
Sparse Core Ops, SparseCore 0:
  83.3 72.9 reduce-scatter.1
where the time goes:
time: 164 us; the launch traced here: 163 us
  waiting for transfers between devices  86.8 us (53%)
  matrix products  33.2 us (20%)
  local copies, waits for them, and re-layouts  25.4 us (15%)
  between operations  13.6 us (8%)
  starting transfers between devices  4.21 us (3%)
    reduce_scatter x1, waiting for transfers between devices, tile_product(): return lax.psum_scatter(rows, 'tile', scatter_dimension=0, tiled=True)  73.2 us
    dot_general x8, matrix products, levels(): jnp.einsum('aeuvwx,awexr->auevr', wide, split, precision=lax.Precision.HI...  20 us
    all_to_all x1, waiting for transfers between devices, tile_product(): lax.all_to_all(coeffs, 'seg', split_axis=0, concat_axis=0, tiled=True)  13.6 us
    another operation x4, local copies, waits for them, and re-layouts, levels(): wide = weights[level].reshape(blocks, stride, 2, K, 2, K)  9.53 us
    another operation x4, local copies, waits for them, and re-layouts  6.42 us
    slice x2, local copies, waits for them, and re-layouts, levels(): wide = weights[level].reshape(blocks, stride, 2, K, 2, K)  5.45 us
    dot_general x1, matrix products, tile_product(): jnp.einsum('nlk,nkr->nlr', expand, coeffs, precision=lax.Precision.HIGHEST)  5.05 us
    dot_general x1, matrix products, tile_product(): jnp.einsum('nkl,nlr->nkr', leaf_proj[0], columns.reshape(BOX, LEAF, width...  4.54 us
  transfers between devices with their start and end apart: 2, of which 2 were waited for; matrix products, arithmetic and copies ran while one was open for 7% of the time, Pallas kernels for 0%

commit v1 on v0

v1 whole, which is shorter than its diff:
```python
import functools

import jax
import jax.numpy as jnp
from jax import lax
from jax.experimental import pallas as pl
from jax.experimental.pallas import tpu as pltpu
from jax.sharding import PartitionSpec as P

F32 = jnp.float32
BF16 = jnp.bfloat16
CHUNK = 128


def split(x):
    hi = x.astype(BF16)
    return hi, (x - hi.astype(F32)).astype(BF16)


def dot(a, b, dims=((1,), (0,))):
    return lax.dot_general(a, b, (dims, ((), ())), preferred_element_type=F32)


def product3(w, v_hi, v_lo):
    w_hi, w_lo = split(w)
    wide = jnp.concatenate([w_hi, w_lo], axis=1)
    tall = jnp.concatenate([v_hi, v_hi], axis=0)
    return dot(wide, tall) + dot(w_hi, v_lo)


def rows_of(ref, start, size):
    return ref[pl.ds(start, size), :]


def pair_step(w, hi, lo, first, second, rank):
    v_hi = jnp.concatenate([rows_of(hi, first, rank), rows_of(hi, second, rank)], axis=0)
    v_lo = jnp.concatenate([rows_of(lo, first, rank), rows_of(lo, second, rank)], axis=0)
    out_hi, out_lo = split(product3(w, v_hi, v_lo))
    for place, half in ((first, 0), (second, 1)):
        hi[pl.ds(place, rank), :] = out_hi[half * rank:(half + 1) * rank]
        lo[pl.ds(place, rank), :] = out_lo[half * rank:(half + 1) * rank]


def column_kernel(n_seg, x_ref, proj_ref, col_ref, mid_ref, *refs):
    outs, (hi, lo) = refs[:n_seg], refs[n_seg:]
    box, rank, leaf = proj_ref.shape
    seg = lax.axis_index("seg")
    for n in range(box):
        x_hi, x_lo = split(x_ref[n * leaf:(n + 1) * leaf, :])
        c_hi, c_lo = split(product3(proj_ref[n], x_hi, x_lo))
        hi[n * rank:(n + 1) * rank, :] = c_hi
        lo[n * rank:(n + 1) * rank, :] = c_lo
    for level in range(col_ref.shape[0]):
        d = 2**level
        for j in range(box // 2):
            first = (j // d) * 2 * d + j % d
            pair_step(col_ref[level, j], hi, lo, first * rank, (first + d) * rank, rank)
    share = box // n_seg
    for delta in reversed(range(n_seg)):
        base = (seg ^ delta) * share
        for p in range(share):
            m_hi, m_lo = split(mid_ref[base + p])
            start = pl.multiple_of((base + p) * rank, rank)
            v_hi, v_lo = rows_of(hi, start, rank), rows_of(lo, start, rank)
            both = dot(jnp.concatenate([m_hi, m_lo], axis=0), v_hi)
            outs[delta][p * rank:(p + 1) * rank, :] = both[:rank] + both[rank:] + dot(m_hi, v_lo)


def row_kernel(n_seg, n_tile, *refs):
    ins, (row_ref, exp_ref, send_ref, keep_ref, hi, lo) = refs[:n_seg], refs[n_seg:]
    box, rank, leaf = exp_ref.shape
    share = box // n_seg
    seg = lax.axis_index("seg")
    tile = lax.axis_index("tile")
    levels = row_ref.shape[0]
    for delta in range(n_seg):
        base = (seg ^ delta) * share
        start = pl.multiple_of(base * rank, share * rank)
        v_hi, v_lo = split(ins[delta][...])
        hi[pl.ds(start, share * rank), :] = v_hi
        lo[pl.ds(start, share * rank), :] = v_lo
    for level in range(levels):
        d = 2**level
        for j in range(box // 2):
            first = (j // d) * 2 * d + j % d
            pair_step(row_ref[level, j], hi, lo, first * rank, (first + d) * rank, rank)
    out_rows = box * leaf // n_tile
    unit = min(out_rows, leaf)
    bits = n_tile.bit_length() - 1
    half = n_tile // 2
    for slot in reversed(range(n_tile)):
        relative = int(format(slot, f"0{bits}b")[::-1], 2)
        block = tile ^ relative
        for piece in range(out_rows // unit):
            n = (block * out_rows + piece * unit) // leaf
            start = pl.multiple_of(n * rank, rank)
            v_hi, v_lo = rows_of(hi, start, rank), rows_of(lo, start, rank)
            e_hi, e_lo = split(exp_ref[n])
            wide = jnp.concatenate([e_hi, e_lo, e_hi], axis=0)
            tall = jnp.concatenate([v_hi, v_hi, v_lo], axis=0)
            out = dot(wide, tall, ((0,), (0,)))
            if unit < leaf:
                parts = leaf // unit
                which = block % parts
                rows = out[:unit]
                for k in range(1, parts):
                    rows = jnp.where(which == k, out[k * unit:(k + 1) * unit], rows)
                out = rows
            target = send_ref if slot >= half else keep_ref
            at = (slot % half) * out_rows + piece * unit
            target[at:at + unit, :] = out


def shards(n_tile, n_seg, right_sides, leaf_proj, col_levels, middle_factor, row_levels, leaf_expand):
    proj, col, mid, row = leaf_proj[0], col_levels[0], middle_factor[0], row_levels[0]
    expand = jnp.swapaxes(leaf_expand[0], 1, 2)
    box, rank, leaf = proj.shape
    width = right_sides.shape[1]
    chunks = width // CHUNK
    out_rows = box * leaf // n_tile
    bits = n_tile.bit_length() - 1
    part = jax.ShapeDtypeStruct((box * rank // n_seg, CHUNK), F32)
    half = jax.ShapeDtypeStruct((box * leaf // 2, CHUNK), F32)
    scratch = [pltpu.VMEM((box * rank, CHUNK), BF16)] * 2
    params = pltpu.CompilerParams(vmem_limit_bytes=24 * 2**20)

    def whole(a):
        return pl.BlockSpec(a.shape, lambda i, r=len(a.shape): (0,) * r)

    def column_side(c):
        return pl.pallas_call(
            functools.partial(column_kernel, n_seg),
            grid=(1,),
            in_specs=[pl.BlockSpec((box * leaf, CHUNK), lambda i: (0, c)), whole(proj), whole(col), whole(mid)],
            out_specs=[whole(part)] * n_seg,
            out_shape=[part] * n_seg,
            scratch_shapes=scratch,
            compiler_params=params,
            cost_estimate=pl.CostEstimate(flops=600_000_000, bytes_accessed=5_000_000, transcendentals=0),
            name="column_side",
        )(right_sides, proj, col, mid)

    def row_side(parts):
        return pl.pallas_call(
            functools.partial(row_kernel, n_seg, n_tile),
            grid=(1,),
            in_specs=[whole(part)] * n_seg + [whole(row), whole(expand)],
            out_specs=[whole(half)] * 2,
            out_shape=[half] * 2,
            scratch_shapes=scratch,
            compiler_params=params,
            cost_estimate=pl.CostEstimate(flops=600_000_000, bytes_accessed=5_000_000, transcendentals=0),
            name="row_side",
        )(*parts, row, expand)

    def swap(x, axis, size, mask):
        return lax.ppermute(x, axis, [(i, i ^ mask) for i in range(size)])

    columns = []
    for c in range(chunks):
        parts = column_side(c)
        columns.append([parts[0]] + [swap(parts[k], "seg", n_seg, k) for k in range(1, n_seg)])
    results = []
    for c in range(chunks):
        send, keep = row_side(columns[c])
        terms = [keep]
        for b in range(bits):
            terms.append(swap(send, "tile", n_tile, 1 << b))
            low = (n_tile >> (b + 2)) * out_rows
            high = 2 * low if b + 1 < bits else out_rows
            send = sum(x[low:high] for x in terms[1:]) + terms[0][low:high]
        results.append(send)
    return jnp.concatenate(results, axis=1)


def solution(mesh):
    in_specs = (
        P(("tile", "seg"), None),
        P("tile", "seg", None, None),
        P("tile", None, "seg", None, None),
        P("tile", "seg", None, None),
        P("tile", None, "seg", None, None),
        P("tile", "seg", None, None),
    )
    out_specs = P(("seg", "tile"), None)
    body = functools.partial(shards, mesh.shape["tile"], mesh.shape["seg"])
    return jax.shard_map(body, mesh=mesh, in_specs=in_specs, out_specs=out_specs, check_vma=False)
```

time: 164 us -> 81.4 us (0.50)
  waiting for transfers between devices: 86.8 us -> 35.3 us
  matrix products: 33.2 us -> 0 us
  starting transfers between devices: 4.21 us -> 25 us
  local copies, waits for them, and re-layouts: 25.4 us -> 5.87 us
  Pallas kernels: 0 us -> 13.8 us
  between operations: 13.6 us -> 0.14 us
    reduce_scatter x1 -> x0, waiting for transfers between devices: 73.2 us -> none  [tile_product(): return lax.psum_scatter(rows, 'tile', scatter_dimension=0, tiled=True)]
    ppermute x0 -> x20, waiting for transfers between devices: none -> 35.3 us  [swap(): return lax.ppermute(x, axis, [(i, i ^ mask) for i in range(size)])]
    dot_general x11 -> x0, matrix products: 33.2 us -> none  [the longest x8 20 us: levels(): jnp.einsum('aeuvwx,awexr->auevr', wide, split, precision=lax.Precision.HI...]
    ppermute x0 -> x20, starting transfers between devices: none -> 25 us  [swap(): return lax.ppermute(x, axis, [(i, i ^ mask) for i in range(size)])]
    another operation x8 -> x0, local copies, waits for them, and re-layouts: 16 us -> none  [the longest x4 9.53 us: levels(): wide = weights[level].reshape(blocks, stride, 2, K, 2, K)]
    pallas_call x0 -> x8, Pallas kernels: none -> 13.8 us  [the longest x4 7.09 us: column_side(): pl.pallas_call(functools.partial(column_kernel, n_seg), grid=(1,), in_spe...]
    all_to_all x1 -> x0, waiting for transfers between devices: 13.6 us -> none  [tile_product(): lax.all_to_all(coeffs, 'seg', split_axis=0, concat_axis=0, tiled=True)]
    slice x2 -> x0, local copies, waits for them, and re-layouts: 5.45 us -> none  [levels(): wide = weights[level].reshape(blocks, stride, 2, K, 2, K)]
  transfers between devices with their start and end apart: 2 -> 20, of which waited for: 2 -> 10; matrix products, arithmetic and copies ran while one was open for 7% -> 0% of each run, Pallas kernels for 0% -> 15%
where the time goes in v1:
time: 81.4 us; the launch traced here: 81.2 us
  waiting for transfers between devices  35.3 us (43%)
  starting transfers between devices  25 us (31%)
  Pallas kernels  13.8 us (17%)
  local copies, waits for them, and re-layouts  5.87 us (7%)
  other arithmetic  1.06 us (1%)
    ppermute x20, waiting for transfers between devices, swap(): return lax.ppermute(x, axis, [(i, i ^ mask) for i in range(size)])  35.3 us
    ppermute x20, starting transfers between devices, swap(): return lax.ppermute(x, axis, [(i, i ^ mask) for i in range(size)])  25 us
    pallas_call x4, Pallas kernels, column_side(): pl.pallas_call(functools.partial(column_kernel, n_seg), grid=(1,), in_spe...  7.09 us
    pallas_call x4, Pallas kernels, row_side(): pl.pallas_call(functools.partial(row_kernel, n_seg, n_tile), grid=(1,), i...  6.74 us
    unnamed x14, local copies, waits for them, and re-layouts  5.87 us
  transfers between devices with their start and end apart: 20, of which 10 were waited for; matrix products, arithmetic and copies ran while one was open for 0% of the time, Pallas kernels for 15%

profile of v1, /device:TPU:0, one launch (start us, length us, event | category | flops | bytes accessed | tf_op | source)
XLA Modules:
  0.0 81.2 jit_solution(1200878875946291532)
XLA Ops:
  0.0 0.0 copy-start
  0.0 2.2 %copy-done = f32[2048,512]{1,0:T(8,128)S(1)} copy-done((f32[2048,512]{1,0:T(8,128)S(1)}, f32[2048,512]{1,0:T(8,128)}, u32[]{:S(2)}) %copy-start) | copy-done | bytes 4194328
  2.2 0.0 copy-start.2
  2.2 1.6 %copy-done.2 = f32[1,4,8,128,128]{4,3,2,1,0:T(8,128)S(1)} copy-done((f32[1,4,8,128,128]{4,3,2,1,0:T(8,128)S(1)}, f32[1,4,8,128,128]{4,3,2,1,0:T(8,128)}, u32[]{:S(2)}) %copy-start.2) | copy-done | bytes 2097176
  3.8 0.0 copy-start.4
  3.8 1.0 %copy-done.4 = f32[1,16,64,128]{3,2,1,0:T(8,128)S(1)} copy-done((f32[1,16,64,128]{3,2,1,0:T(8,128)S(1)}, f32[1,16,64,128]{3,2,1,0:T(8,128)}, u32[]{:S(2)}) %copy-start.4) | copy-done | bytes 524312
  4.8 0.0 copy-start.5
  4.8 1.0 %copy-done.5 = f32[1,16,64,64]{3,2,1,0:T(8,128)S(1)} copy-done((f32[1,16,64,64]{3,2,1,0:T(8,128)S(1)}, f32[1,16,64,64]{3,2,1,0:T(8,128)}, u32[]{:S(2)}) %copy-start.5) | copy-done | bytes 262168
  5.9 1.8 %column_side.4 = (f32[512,128]{1,0:T(8,128)S(1)}, f32[512,128]{1,0:T(8,128)S(1)}) custom-call(f32[2048,512]{1,0:T(8,128)S(1)} %copy-done, f32[16,64,128]{2,1,0:T(8,128)S(1)} %bitcast.15, f32[4,8,128,128]{3,2,1,0:T(8,128)S(1)} %bitcast.7, f32[16,64,64]{2,1,0:T(8,128)S(1)} %bitcast.19), custom_call_target="tpu_custom_call" | custom-call | flops 600000000 | bytes 5000000 | tf_op jit(solution)/shard_map/column_side/pallas_call | solution.py:131
  7.6 0.0 copy-start.3
  7.6 0.0 copy-start.6
  7.6 3.0 %collective-permute-start = (f32[512,128]{1,0:T(8,128)S(1)}, f32[512,128]{1,0:T(8,128)S(1)}, u32[]{:S(2)}, u32[]{:S(2)}) collective-permute-start(f32[512,128]{1,0:T(8,128)S(1)} %get-tuple-element.22), channel_id=1, source_target_pairs={{0,1},{1,0},{2,3},{3,2},{4,5},{5,4},{6,7},{7,6},{8,9},{9,8},{10,11... | collective-permute-start | bytes 786440 | tf_op jit(solution)/shard_map/ppermute | solution.py:157
  10.7 0.0 copy-start.1
  10.7 1.8 %column_side.5 = (f32[512,128]{1,0:T(8,128)S(1)}, f32[512,128]{1,0:T(8,128)S(1)}) custom-call(f32[2048,512]{1,0:T(8,128)S(1)} %copy-done, f32[16,64,128]{2,1,0:T(8,128)S(1)} %bitcast.16, f32[4,8,128,128]{3,2,1,0:T(8,128)S(1)} %bitcast.8, f32[16,64,64]{2,1,0:T(8,128)S(1)} %bitcast.20), custom_call_target="tpu_custom_call" | custom-call | flops 600000000 | bytes 5000000 | tf_op jit(solution)/shard_map/column_side/pallas_call | solution.py:131
  12.4 0.1 collective-permute-start.5
  12.5 5.3 %collective-permute-done.refs_1_ = f32[512,128]{1,0:T(8,128)S(1)} collective-permute-done((f32[512,128]{1,0:T(8,128)S(1)}, f32[512,128]{1,0:T(8,128)S(1)}, u32[]{:S(2)}, u32[]{:S(2)}) %collective-permute-start) | collective-permute-done | bytes 262176 | tf_op jit(solution)/shard_map/ppermute | solution.py:157
  17.8 0.0 copy-done.3
  17.8 0.0 copy-done.6
  17.8 1.6 %row_side.4 = (f32[1024,128]{1,0:T(8,128)S(1)}, f32[1024,128]{1,0:T(8,128)S(1)}) custom-call(f32[512,128]{1,0:T(8,128)S(1)} %get-tuple-element.21.refs_0_, f32[512,128]{1,0:T(8,128)S(1)} %collective-permute-done.refs_1_, f32[4,8,128,128]{3,2,1,0:T(8,128)S(1)} %bitcast.11, f32[16,64,128]{2,1,0:T(8,128)S(1)} %bitcast.23), custom_call_target="tpu_custom_call" | custom-call | flops 600000000 | bytes 5000000 | tf_op jit(solution)/shard_map/row_side/pallas_call | solution.py:144
  19.4 0.1 collective-permute-start.1
  19.5 0.0 copy-done.1
  19.5 1.8 %column_side.6 = (f32[512,128]{1,0:T(8,128)S(1)}, f32[512,128]{1,0:T(8,128)S(1)}) custom-call(f32[2048,512]{1,0:T(8,128)S(1)} %copy-done.1, f32[16,64,128]{2,1,0:T(8,128)S(1)} %bitcast.17, f32[4,8,128,128]{3,2,1,0:T(8,128)S(1)} %bitcast.9, f32[16,64,64]{2,1,0:T(8,128)S(1)} %bitcast.21), custom_call_target="tpu_custom_call" | custom-call | flops 600000000 | bytes 5000000 | tf_op jit(solution)/shard_map/column_side/pallas_call | solution.py:131
  21.3 2.1 %collective-permute-start.10 = (f32[512,128]{1,0:T(8,128)S(1)}, f32[512,128]{1,0:T(8,128)S(1)}, u32[]{:S(2)}, u32[]{:S(2)}) collective-permute-start(f32[512,128]{1,0:T(8,128)S(1)} %get-tuple-element.30), channel_id=1, source_target_pairs={{0,1},{1,0},{2,3},{3,2},{4,5},{5,4},{6,7},{7,6},{8,9},{9,8},{10,11... | collective-permute-start | bytes 786440 | tf_op jit(solution)/shard_map/ppermute | solution.py:157
  23.4 1.8 %column_side.7 = (f32[512,128]{1,0:T(8,128)S(1)}, f32[512,128]{1,0:T(8,128)S(1)}) custom-call(f32[2048,512]{1,0:T(8,128)S(1)} %copy-done.1, f32[16,64,128]{2,1,0:T(8,128)S(1)} %bitcast.18, f32[4,8,128,128]{3,2,1,0:T(8,128)S(1)} %bitcast.10, f32[16,64,64]{2,1,0:T(8,128)S(1)} %bitcast.22), custom_call_target="tpu_custom_call" | custom-call | flops 600000000 | bytes 5000000 | tf_op jit(solution)/shard_map/column_side/pallas_call | solution.py:131
  25.2 0.1 collective-permute-start.15
  25.2 0.0 collective-permute-done.5.refs_1_
  25.2 1.6 %row_side.5 = (f32[1024,128]{1,0:T(8,128)S(1)}, f32[1024,128]{1,0:T(8,128)S(1)}) custom-call(f32[512,128]{1,0:T(8,128)S(1)} %get-tuple-element.25.refs_0_, f32[512,128]{1,0:T(8,128)S(1)} %collective-permute-done.5.refs_1_, f32[4,8,128,128]{3,2,1,0:T(8,128)S(1)} %bitcast.12, f32[16,64,128]{2,1,0:T(8,128)S(1)} %bitcast.24), custom_call_target="tpu_custom_call" | custom-call | flops 600000000 | bytes 5000000 | tf_op jit(solution)/shard_map/row_side/pallas_call | solution.py:144
  26.9 0.3 collective-permute-start.6
  27.2 3.4 %collective-permute-done.10.refs_1_ = f32[512,128]{1,0:T(8,128)S(1)} collective-permute-done((f32[512,128]{1,0:T(8,128)S(1)}, f32[512,128]{1,0:T(8,128)S(1)}, u32[]{:S(2)}, u32[]{:S(2)}) %collective-permute-start.10) | collective-permute-done | bytes 262176 | tf_op jit(solution)/shard_map/ppermute | solution.py:157
  30.6 1.6 %row_side.6 = (f32[1024,128]{1,0:T(8,128)S(1)}, f32[1024,128]{1,0:T(8,128)S(1)}) custom-call(f32[512,128]{1,0:T(8,128)S(1)} %get-tuple-element.29.refs_0_, f32[512,128]{1,0:T(8,128)S(1)} %collective-permute-done.10.refs_1_, f32[4,8,128,128]{3,2,1,0:T(8,128)S(1)} %bitcast.13, f32[16,64,128]{2,1,0:T(8,128)S(1)} %bitcast.25), custom_call_target="tpu_custom_call" | custom-call | flops 600000000 | bytes 5000000 | tf_op jit(solution)/shard_map/row_side/pallas_call | solution.py:144
  32.2 0.1 collective-permute-start.11
  32.3 3.7 %collective-permute-done.15.refs_1_ = f32[512,128]{1,0:T(8,128)S(1)} collective-permute-done((f32[512,128]{1,0:T(8,128)S(1)}, f32[512,128]{1,0:T(8,128)S(1)}, u32[]{:S(2)}, u32[]{:S(2)}) %collective-permute-start.15) | collective-permute-done | bytes 262176 | tf_op jit(solution)/shard_map/ppermute | solution.py:157
  36.0 1.8 %row_side.7 = (f32[1024,128]{1,0:T(8,128)S(1)}, f32[1024,128]{1,0:T(8,128)S(1)}) custom-call(f32[512,128]{1,0:T(8,128)S(1)} %get-tuple-element.33.refs_0_, f32[512,128]{1,0:T(8,128)S(1)} %collective-permute-done.15.refs_1_, f32[4,8,128,128]{3,2,1,0:T(8,128)S(1)} %bitcast.14, f32[16,64,128]{2,1,0:T(8,128)S(1)} %bitcast.26), custom_call_target="tpu_custom_call" | custom-call | flops 600000000 | bytes 5000000 | tf_op jit(solution)/shard_map/row_side/pallas_call | solution.py:144
  37.8 0.1 collective-permute-start.16
  37.9 0.0 collective-permute-done.1
  37.9 1.8 %collective-permute-start.2 = (f32[512,128]{1,0:T(8,128)S(1)}, f32[512,128]{1,0:T(8,128)S(1)}, u32[]{:S(2)}, u32[]{:S(2)}) collective-permute-start(f32[512,128]{1,0:T(8,128)S(1)} %slice_add_fusion.3), channel_id=1, source_target_pairs={{0,4},{2,6},{4,0},{6,2},{8,12},{10,14},{12,8},{14,10},{16,20},{18,... | collective-permute-start | bytes 786440 | tf_op jit(solution)/shard_map/ppermute | solution.py:157
  39.8 0.0 collective-permute-done.6
  39.8 0.3 collective-permute-start.7
  40.1 0.0 collective-permute-done.11
  40.2 1.8 %collective-permute-start.12 = (f32[512,128]{1,0:T(8,128)S(1)}, f32[512,128]{1,0:T(8,128)S(1)}, u32[]{:S(2)}, u32[]{:S(2)}) collective-permute-start(f32[512,128]{1,0:T(8,128)S(1)} %slice_add_fusion.1), channel_id=1, source_target_pairs={{0,4},{2,6},{4,0},{6,2},{8,12},{10,14},{12,8},{14,10},{16,20},{18,... | collective-permute-start | bytes 786440 | tf_op jit(solution)/shard_map/ppermute | solution.py:157
  42.0 0.0 collective-permute-done.16
  42.0 0.3 collective-permute-start.17
  42.4 4.7 %collective-permute-done.2 = f32[512,128]{1,0:T(8,128)S(1)} collective-permute-done((f32[512,128]{1,0:T(8,128)S(1)}, f32[512,128]{1,0:T(8,128)S(1)}, u32[]{:S(2)}, u32[]{:S(2)}) %collective-permute-start.2) | collective-permute-done | bytes 262176 | tf_op jit(solution)/shard_map/ppermute | solution.py:157
  47.1 1.9 %collective-permute-start.3 = (f32[256,128]{1,0:T(8,128)S(1)}, f32[256,128]{1,0:T(8,128)S(1)}, u32[]{:S(2)}, u32[]{:S(2)}) collective-permute-start(f32[256,128]{1,0:T(8,128)S(1)} %fusion.3), channel_id=1, source_target_pairs={{0,8},{2,10},{4,12},{6,14},{8,0},{10,2},{12,4},{14,6},{16,24},{18,... | collective-permute-start | bytes 393224 | tf_op jit(solution)/shard_map/ppermute | solution.py:157
  49.0 3.7 %collective-permute-done.7 = f32[512,128]{1,0:T(8,128)S(1)} collective-permute-done((f32[512,128]{1,0:T(8,128)S(1)}, f32[512,128]{1,0:T(8,128)S(1)}, u32[]{:S(2)}, u32[]{:S(2)}) %collective-permute-start.7) | collective-permute-done | bytes 262176 | tf_op jit(solution)/shard_map/ppermute | solution.py:157
  52.8 1.9 %collective-permute-start.8 = (f32[256,128]{1,0:T(8,128)S(1)}, f32[256,128]{1,0:T(8,128)S(1)}, u32[]{:S(2)}, u32[]{:S(2)}) collective-permute-start(f32[256,128]{1,0:T(8,128)S(1)} %fusion.2), channel_id=1, source_target_pairs={{0,8},{2,10},{4,12},{6,14},{8,0},{10,2},{12,4},{14,6},{16,24},{18,... | collective-permute-start | bytes 393224 | tf_op jit(solution)/shard_map/ppermute | solution.py:157
  54.6 3.7 %collective-permute-done.12 = f32[512,128]{1,0:T(8,128)S(1)} collective-permute-done((f32[512,128]{1,0:T(8,128)S(1)}, f32[512,128]{1,0:T(8,128)S(1)}, u32[]{:S(2)}, u32[]{:S(2)}) %collective-permute-start.12) | collective-permute-done | bytes 262176 | tf_op jit(solution)/shard_map/ppermute | solution.py:157
  58.4 1.9 %collective-permute-start.13 = (f32[256,128]{1,0:T(8,128)S(1)}, f32[256,128]{1,0:T(8,128)S(1)}, u32[]{:S(2)}, u32[]{:S(2)}) collective-permute-start(f32[256,128]{1,0:T(8,128)S(1)} %fusion.1), channel_id=1, source_target_pairs={{0,8},{2,10},{4,12},{6,14},{8,0},{10,2},{12,4},{14,6},{16,24},{18,... | collective-permute-start | bytes 393224 | tf_op jit(solution)/shard_map/ppermute | solution.py:157
  60.3 3.3 %collective-permute-done.17 = f32[512,128]{1,0:T(8,128)S(1)} collective-permute-done((f32[512,128]{1,0:T(8,128)S(1)}, f32[512,128]{1,0:T(8,128)S(1)}, u32[]{:S(2)}, u32[]{:S(2)}) %collective-permute-start.17) | collective-permute-done | bytes 262176 | tf_op jit(solution)/shard_map/ppermute | solution.py:157
  63.6 1.9 %collective-permute-start.18 = (f32[256,128]{1,0:T(8,128)S(1)}, f32[256,128]{1,0:T(8,128)S(1)}, u32[]{:S(2)}, u32[]{:S(2)}) collective-permute-start(f32[256,128]{1,0:T(8,128)S(1)} %fusion), channel_id=1, source_target_pairs={{0,8},{2,10},{4,12},{6,14},{8,0},{10,2},{12,4},{14,6},{16,24},{18,... | collective-permute-start | bytes 393224 | tf_op jit(solution)/shard_map/ppermute | solution.py:157
  65.5 0.0 collective-permute-done.3
  65.5 2.7 %collective-permute-start.4 = (f32[128,128]{1,0:T(8,128)S(1)}, f32[128,128]{1,0:T(8,128)S(1)}, u32[]{:S(2)}, u32[]{:S(2)}) collective-permute-start(f32[128,128]{1,0:T(8,128)S(1)} %fusion.13), channel_id=1, source_target_pairs={{0,16},{2,18},{4,20},{6,22},{8,24},{10,26},{12,28},{14,30},{16,0},... | collective-permute-start | bytes 196616 | tf_op jit(solution)/shard_map/ppermute | solution.py:157
  68.2 0.0 collective-permute-done.8
  68.2 0.4 collective-permute-start.9
  68.6 0.0 collective-permute-done.13
  68.6 2.7 %collective-permute-start.14 = (f32[128,128]{1,0:T(8,128)S(1)}, f32[128,128]{1,0:T(8,128)S(1)}, u32[]{:S(2)}, u32[]{:S(2)}) collective-permute-start(f32[128,128]{1,0:T(8,128)S(1)} %fusion.7), channel_id=1, source_target_pairs={{0,16},{2,18},{4,20},{6,22},{8,24},{10,26},{12,28},{14,30},{16,0},... | collective-permute-start | bytes 196616 | tf_op jit(solution)/shard_map/ppermute | solution.py:157
  71.3 0.0 collective-permute-done.18
  71.3 1.7 %collective-permute-start.19 = (f32[128,128]{1,0:T(8,128)S(1)}, f32[128,128]{1,0:T(8,128)S(1)}, u32[]{:S(2)}, u32[]{:S(2)}) collective-permute-start(f32[128,128]{1,0:T(8,128)S(1)} %fusion.4), channel_id=1, source_target_pairs={{0,16},{2,18},{4,20},{6,22},{8,24},{10,26},{12,28},{14,30},{16,0},... | collective-permute-start | bytes 196616 | tf_op jit(solution)/shard_map/ppermute | solution.py:157
  73.0 0.0 collective-permute-done.4
  73.0 5.2 %collective-permute-done.9 = f32[128,128]{1,0:T(8,128)S(1)} collective-permute-done((f32[128,128]{1,0:T(8,128)S(1)}, f32[128,128]{1,0:T(8,128)S(1)}, u32[]{:S(2)}, u32[]{:S(2)}) %collective-permute-start.9) | collective-permute-done | bytes 65568 | tf_op jit(solution)/shard_map/ppermute | solution.py:157
  78.2 1.4 %collective-permute-done.14 = f32[128,128]{1,0:T(8,128)S(1)} collective-permute-done((f32[128,128]{1,0:T(8,128)S(1)}, f32[128,128]{1,0:T(8,128)S(1)}, u32[]{:S(2)}, u32[]{:S(2)}) %collective-permute-start.14) | collective-permute-done | bytes 65568 | tf_op jit(solution)/shard_map/ppermute | solution.py:157
  79.6 0.8 collective-permute-done.19
  80.4 0.7 pad_maximum_fusion
  (16 shorter events, 0.3 us)
Async XLA Ops:
  0.0 2.2 %copy-start = (f32[2048,512]{1,0:T(8,128)S(1)}, f32[2048,512]{1,0:T(8,128)}, u32[]{:S(2)}) copy-start(f32[2048,512]{1,0:T(8,128)} %x_ref.7) | copy-start | bytes 12582916
  2.2 1.6 %copy-start.2 = (f32[1,4,8,128,128]{4,3,2,1,0:T(8,128)S(1)}, f32[1,4,8,128,128]{4,3,2,1,0:T(8,128)}, u32[]{:S(2)}) copy-start(f32[1,4,8,128,128]{4,3,2,1,0:T(8,128)} %param.8) | copy-start | bytes 6291460
  3.8 1.0 %copy-start.4 = (f32[1,16,64,128]{3,2,1,0:T(8,128)S(1)}, f32[1,16,64,128]{3,2,1,0:T(8,128)}, u32[]{:S(2)}) copy-start(f32[1,16,64,128]{3,2,1,0:T(8,128)} %param.7) | copy-start | bytes 1572868
  4.8 1.0 %copy-start.5 = (f32[1,16,64,64]{3,2,1,0:T(8,128)S(1)}, f32[1,16,64,64]{3,2,1,0:T(8,128)}, u32[]{:S(2)}) copy-start(f32[1,16,64,64]{3,2,1,0:T(8,128)} %param.9) | copy-start | bytes 786436
  7.6 10.2 %copy-start.3 = (f32[1,4,8,128,128]{4,3,2,1,0:T(8,128)S(1)}, f32[1,4,8,128,128]{4,3,2,1,0:T(8,128)}, u32[]{:S(2)}) copy-start(f32[1,4,8,128,128]{4,3,2,1,0:T(8,128)} %param.10) | copy-start | bytes 6291460
  7.6 10.2 %copy-start.6 = (f32[1,16,128,64]{2,3,1,0:T(8,128)S(1)}, f32[1,16,128,64]{2,3,1,0:T(8,128)}, u32[]{:S(2)}) copy-start(f32[1,16,128,64]{2,3,1,0:T(8,128)} %param.11) | copy-start | bytes 1572868
  7.6 10.1 %collective-permute-start = (f32[512,128]{1,0:T(8,128)S(1)}, f32[512,128]{1,0:T(8,128)S(1)}, u32[]{:S(2)}, u32[]{:S(2)}) collective-permute-start(f32[512,128]{1,0:T(8,128)S(1)} %get-tuple-element.22), channel_id=1, source_target_pairs={{0,1},{1,0},{2,3},{3,2},{4,5},{5,4},{6,7},{7,6},{8,9},{9,8},{10,11... | collective-permute-start | bytes 786440 | tf_op jit(solution)/shard_map/ppermute | solution.py:157
  10.7 8.9 %copy-start.1 = (f32[2048,512]{1,0:T(8,128)S(1)}, f32[2048,512]{1,0:T(8,128)}, u32[]{:S(2)}) copy-start(f32[2048,512]{1,0:T(8,128)} %x_ref.7) | copy-start | bytes 12582916
  12.4 12.8 %collective-permute-start.5 = (f32[512,128]{1,0:T(8,128)S(1)}, f32[512,128]{1,0:T(8,128)S(1)}, u32[]{:S(2)}, u32[]{:S(2)}) collective-permute-start(f32[512,128]{1,0:T(8,128)S(1)} %get-tuple-element.26), channel_id=1, source_target_pairs={{0,1},{1,0},{2,3},{3,2},{4,5},{5,4},{6,7},{7,6},{8,9},{9,8},{10,11... | collective-permute-start | bytes 786440 | tf_op jit(solution)/shard_map/ppermute | solution.py:157
  19.4 18.5 %collective-permute-start.1 = (f32[1024,128]{1,0:T(8,128)S(1)}, f32[1024,128]{1,0:T(8,128)S(1)}, u32[]{:S(2)}, u32[]{:S(2)}) collective-permute-start(f32[1024,128]{1,0:T(8,128)S(1)} %get-tuple-element.23), channel_id=1, source_target_pairs={{0,2},{2,0},{4,6},{6,4},{8,10},{10,8},{12,14},{14,12},{16,18},{18,... | collective-permute-start | bytes 1572872 | tf_op jit(solution)/shard_map/ppermute | solution.py:157
  21.3 9.3 %collective-permute-start.10 = (f32[512,128]{1,0:T(8,128)S(1)}, f32[512,128]{1,0:T(8,128)S(1)}, u32[]{:S(2)}, u32[]{:S(2)}) collective-permute-start(f32[512,128]{1,0:T(8,128)S(1)} %get-tuple-element.30), channel_id=1, source_target_pairs={{0,1},{1,0},{2,3},{3,2},{4,5},{5,4},{6,7},{7,6},{8,9},{9,8},{10,11... | collective-permute-start | bytes 786440 | tf_op jit(solution)/shard_map/ppermute | solution.py:157
  25.2 10.8 %collective-permute-start.15 = (f32[512,128]{1,0:T(8,128)S(1)}, f32[512,128]{1,0:T(8,128)S(1)}, u32[]{:S(2)}, u32[]{:S(2)}) collective-permute-start(f32[512,128]{1,0:T(8,128)S(1)} %get-tuple-element.34), channel_id=1, source_target_pairs={{0,1},{1,0},{2,3},{3,2},{4,5},{5,4},{6,7},{7,6},{8,9},{9,8},{10,11... | collective-permute-start | bytes 786440 | tf_op jit(solution)/shard_map/ppermute | solution.py:157
  26.9 12.9 %collective-permute-start.6 = (f32[1024,128]{1,0:T(8,128)S(1)}, f32[1024,128]{1,0:T(8,128)S(1)}, u32[]{:S(2)}, u32[]{:S(2)}) collective-permute-start(f32[1024,128]{1,0:T(8,128)S(1)} %get-tuple-element.27), channel_id=1, source_target_pairs={{0,2},{2,0},{4,6},{6,4},{8,10},{10,8},{12,14},{14,12},{16,18},{18,... | collective-permute-start | bytes 1572872 | tf_op jit(solution)/shard_map/ppermute | solution.py:157
  32.2 7.9 %collective-permute-start.11 = (f32[1024,128]{1,0:T(8,128)S(1)}, f32[1024,128]{1,0:T(8,128)S(1)}, u32[]{:S(2)}, u32[]{:S(2)}) collective-permute-start(f32[1024,128]{1,0:T(8,128)S(1)} %get-tuple-element.31), channel_id=1, source_target_pairs={{0,2},{2,0},{4,6},{6,4},{8,10},{10,8},{12,14},{14,12},{16,18},{18,... | collective-permute-start | bytes 1572872 | tf_op jit(solution)/shard_map/ppermute | solution.py:157
  37.8 4.2 %collective-permute-start.16 = (f32[1024,128]{1,0:T(8,128)S(1)}, f32[1024,128]{1,0:T(8,128)S(1)}, u32[]{:S(2)}, u32[]{:S(2)}) collective-permute-start(f32[1024,128]{1,0:T(8,128)S(1)} %get-tuple-element.35), channel_id=1, source_target_pairs={{0,2},{2,0},{4,6},{6,4},{8,10},{10,8},{12,14},{14,12},{16,18},{18,... | collective-permute-start | bytes 1572872 | tf_op jit(solution)/shard_map/ppermute | solution.py:157
  37.9 9.2 %collective-permute-start.2 = (f32[512,128]{1,0:T(8,128)S(1)}, f32[512,128]{1,0:T(8,128)S(1)}, u32[]{:S(2)}, u32[]{:S(2)}) collective-permute-start(f32[512,128]{1,0:T(8,128)S(1)} %slice_add_fusion.3), channel_id=1, source_target_pairs={{0,4},{2,6},{4,0},{6,2},{8,12},{10,14},{12,8},{14,10},{16,20},{18,... | collective-permute-start | bytes 786440 | tf_op jit(solution)/shard_map/ppermute | solution.py:157
  39.8 12.9 %collective-permute-start.7 = (f32[512,128]{1,0:T(8,128)S(1)}, f32[512,128]{1,0:T(8,128)S(1)}, u32[]{:S(2)}, u32[]{:S(2)}) collective-permute-start(f32[512,128]{1,0:T(8,128)S(1)} %slice_add_fusion.2), channel_id=1, source_target_pairs={{0,4},{2,6},{4,0},{6,2},{8,12},{10,14},{12,8},{14,10},{16,20},{18,... | collective-permute-start | bytes 786440 | tf_op jit(solution)/shard_map/ppermute | solution.py:157
  40.2 18.2 %collective-permute-start.12 = (f32[512,128]{1,0:T(8,128)S(1)}, f32[512,128]{1,0:T(8,128)S(1)}, u32[]{:S(2)}, u32[]{:S(2)}) collective-permute-start(f32[512,128]{1,0:T(8,128)S(1)} %slice_add_fusion.1), channel_id=1, source_target_pairs={{0,4},{2,6},{4,0},{6,2},{8,12},{10,14},{12,8},{14,10},{16,20},{18,... | collective-permute-start | bytes 786440 | tf_op jit(solution)/shard_map/ppermute | solution.py:157
  42.0 21.5 %collective-permute-start.17 = (f32[512,128]{1,0:T(8,128)S(1)}, f32[512,128]{1,0:T(8,128)S(1)}, u32[]{:S(2)}, u32[]{:S(2)}) collective-permute-start(f32[512,128]{1,0:T(8,128)S(1)} %slice_add_fusion), channel_id=1, source_target_pairs={{0,4},{2,6},{4,0},{6,2},{8,12},{10,14},{12,8},{14,10},{16,20},{18,... | collective-permute-start | bytes 786440 | tf_op jit(solution)/shard_map/ppermute | solution.py:157
  47.1 18.3 %collective-permute-start.3 = (f32[256,128]{1,0:T(8,128)S(1)}, f32[256,128]{1,0:T(8,128)S(1)}, u32[]{:S(2)}, u32[]{:S(2)}) collective-permute-start(f32[256,128]{1,0:T(8,128)S(1)} %fusion.3), channel_id=1, source_target_pairs={{0,8},{2,10},{4,12},{6,14},{8,0},{10,2},{12,4},{14,6},{16,24},{18,... | collective-permute-start | bytes 393224 | tf_op jit(solution)/shard_map/ppermute | solution.py:157
  52.8 15.4 %collective-permute-start.8 = (f32[256,128]{1,0:T(8,128)S(1)}, f32[256,128]{1,0:T(8,128)S(1)}, u32[]{:S(2)}, u32[]{:S(2)}) collective-permute-start(f32[256,128]{1,0:T(8,128)S(1)} %fusion.2), channel_id=1, source_target_pairs={{0,8},{2,10},{4,12},{6,14},{8,0},{10,2},{12,4},{14,6},{16,24},{18,... | collective-permute-start | bytes 393224 | tf_op jit(solution)/shard_map/ppermute | solution.py:157
  58.4 10.2 %collective-permute-start.13 = (f32[256,128]{1,0:T(8,128)S(1)}, f32[256,128]{1,0:T(8,128)S(1)}, u32[]{:S(2)}, u32[]{:S(2)}) collective-permute-start(f32[256,128]{1,0:T(8,128)S(1)} %fusion.1), channel_id=1, source_target_pairs={{0,8},{2,10},{4,12},{6,14},{8,0},{10,2},{12,4},{14,6},{16,24},{18,... | collective-permute-start | bytes 393224 | tf_op jit(solution)/shard_map/ppermute | solution.py:157
  63.6 7.6 %collective-permute-start.18 = (f32[256,128]{1,0:T(8,128)S(1)}, f32[256,128]{1,0:T(8,128)S(1)}, u32[]{:S(2)}, u32[]{:S(2)}) collective-permute-start(f32[256,128]{1,0:T(8,128)S(1)} %fusion), channel_id=1, source_target_pairs={{0,8},{2,10},{4,12},{6,14},{8,0},{10,2},{12,4},{14,6},{16,24},{18,... | collective-permute-start | bytes 393224 | tf_op jit(solution)/shard_map/ppermute | solution.py:157
  65.5 7.5 %collective-permute-start.4 = (f32[128,128]{1,0:T(8,128)S(1)}, f32[128,128]{1,0:T(8,128)S(1)}, u32[]{:S(2)}, u32[]{:S(2)}) collective-permute-start(f32[128,128]{1,0:T(8,128)S(1)} %fusion.13), channel_id=1, source_target_pairs={{0,16},{2,18},{4,20},{6,22},{8,24},{10,26},{12,28},{14,30},{16,0},... | collective-permute-start | bytes 196616 | tf_op jit(solution)/shard_map/ppermute | solution.py:157
  68.2 10.0 %collective-permute-start.9 = (f32[128,128]{1,0:T(8,128)S(1)}, f32[128,128]{1,0:T(8,128)S(1)}, u32[]{:S(2)}, u32[]{:S(2)}) collective-permute-start(f32[128,128]{1,0:T(8,128)S(1)} %fusion.10), channel_id=1, source_target_pairs={{0,16},{2,18},{4,20},{6,22},{8,24},{10,26},{12,28},{14,30},{16,0},... | collective-permute-start | bytes 196616 | tf_op jit(solution)/shard_map/ppermute | solution.py:157
  68.6 11.0 %collective-permute-start.14 = (f32[128,128]{1,0:T(8,128)S(1)}, f32[128,128]{1,0:T(8,128)S(1)}, u32[]{:S(2)}, u32[]{:S(2)}) collective-permute-start(f32[128,128]{1,0:T(8,128)S(1)} %fusion.7), channel_id=1, source_target_pairs={{0,16},{2,18},{4,20},{6,22},{8,24},{10,26},{12,28},{14,30},{16,0},... | collective-permute-start | bytes 196616 | tf_op jit(solution)/shard_map/ppermute | solution.py:157
  71.3 9.1 %collective-permute-start.19 = (f32[128,128]{1,0:T(8,128)S(1)}, f32[128,128]{1,0:T(8,128)S(1)}, u32[]{:S(2)}, u32[]{:S(2)}) collective-permute-start(f32[128,128]{1,0:T(8,128)S(1)} %fusion.4), channel_id=1, source_target_pairs={{0,16},{2,18},{4,20},{6,22},{8,24},{10,26},{12,28},{14,30},{16,0},... | collective-permute-start | bytes 196616 | tf_op jit(solution)/shard_map/ppermute | solution.py:157

commit v2 on v1

v2 whole, which is shorter than its diff:
```python
import functools

import jax
import jax.numpy as jnp
from jax import lax
from jax.experimental import pallas as pl
from jax.experimental.pallas import tpu as pltpu
from jax.sharding import PartitionSpec as P

F32 = jnp.float32
BF16 = jnp.bfloat16
CHUNK = 128


def split(x):
    hi = x.astype(BF16)
    return hi, (x - hi.astype(F32)).astype(BF16)


def dot(a, b, dims=((1,), (0,))):
    return lax.dot_general(a, b, (dims, ((), ())), preferred_element_type=F32)


def wide_of(w):
    return jnp.concatenate(split(w), axis=1)


def product3(wide, v_hi, v_lo):
    tall = jnp.concatenate([v_hi, v_hi], axis=0)
    return dot(wide, tall) + dot(wide[:, :v_hi.shape[0]], v_lo)


def rows_of(ref, start, size):
    return ref[pl.ds(start, size), :]


def level_step(level, wide_at, hi, lo, rank):
    d = 2**level
    for j in range(hi.shape[0] // (2 * rank)):
        first = ((j // d) * 2 * d + j % d) * rank
        second = first + d * rank
        v_hi = jnp.concatenate([rows_of(hi, first, rank), rows_of(hi, second, rank)], axis=0)
        v_lo = jnp.concatenate([rows_of(lo, first, rank), rows_of(lo, second, rank)], axis=0)
        out_hi, out_lo = split(product3(wide_at(j), v_hi, v_lo))
        for place, half in ((first, 0), (second, 1)):
            hi[pl.ds(place, rank), :] = out_hi[half * rank:(half + 1) * rank]
            lo[pl.ds(place, rank), :] = out_lo[half * rank:(half + 1) * rank]


def column_kernel(n_seg, start, x_hbm, proj_hbm, col_hbm, mid_hbm, *refs):
    outs, (x_ref, proj_ref, col_ref, mid_ref, hi, lo, sems) = refs[:-7], refs[-7:]
    box, rank, leaf = proj_ref.shape
    levels = col_ref.shape[0]
    width = x_ref.shape[1]
    pieces = 4
    per = box // pieces
    share = box // n_seg
    seg = lax.axis_index("seg")

    def x_copy(k):
        rows = pl.ds(k * per * leaf, per * leaf)
        return pltpu.make_async_copy(x_hbm.at[rows, pl.ds(start, width)], x_ref.at[rows, :], sems.at[k])

    proj_copy = pltpu.make_async_copy(proj_hbm, proj_ref, sems.at[pieces])
    col_copies = [pltpu.make_async_copy(col_hbm.at[k], col_ref.at[k], sems.at[pieces + 1 + k]) for k in range(levels)]
    mid_copy = pltpu.make_async_copy(mid_hbm, mid_ref, sems.at[pieces + 1 + levels])
    proj_copy.start()
    for k in range(pieces):
        x_copy(k).start()
    for copy in col_copies:
        copy.start()
    mid_copy.start()

    proj_copy.wait()
    for k in range(pieces):
        x_copy(k).wait()
        for n in range(k * per, (k + 1) * per):
            x_hi, x_lo = split(x_ref[n * leaf:(n + 1) * leaf, :])
            c_hi, c_lo = split(product3(wide_of(proj_ref[n]), x_hi, x_lo))
            hi[n * rank:(n + 1) * rank, :] = c_hi
            lo[n * rank:(n + 1) * rank, :] = c_lo
    for level in range(levels):
        col_copies[level].wait()
        level_step(level, lambda j: wide_of(col_ref[level, j]), hi, lo, rank)
    mid_copy.wait()
    for delta in reversed(range(n_seg)):
        base = (seg ^ delta) * share
        for p in range(share):
            m_hi, m_lo = split(mid_ref[base + p])
            at = pl.multiple_of((base + p) * rank, rank)
            v_hi, v_lo = rows_of(hi, at, rank), rows_of(lo, at, rank)
            both = dot(jnp.concatenate([m_hi, m_lo], axis=0), v_hi)
            out = both[:rank] + both[rank:] + dot(m_hi, v_lo)
            for k in range(width // CHUNK):
                outs[k * n_seg + delta][p * rank:(p + 1) * rank, :] = out[:, k * CHUNK:(k + 1) * CHUNK]


def weights_kernel(after_ref, row_ref, exp_ref, wide_ref, tall_ref):
    del after_ref
    for level in range(row_ref.shape[0]):
        for j in range(row_ref.shape[1]):
            wide_ref[level, j] = wide_of(row_ref[level, j])
    for n in range(exp_ref.shape[0]):
        e_hi, e_lo = split(exp_ref[n])
        tall_ref[n] = jnp.concatenate([e_hi, e_lo, e_hi], axis=0)


def row_kernel(n_seg, n_tile, leaf, *refs):
    ins, (row_ref, exp_ref, send_ref, keep_ref, hi, lo) = refs[:n_seg], refs[n_seg:]
    box = exp_ref.shape[0]
    rank = hi.shape[0] // box
    share = box // n_seg
    seg = lax.axis_index("seg")
    tile = lax.axis_index("tile")
    for delta in range(n_seg):
        base = (seg ^ delta) * share
        at = pl.multiple_of(base * rank, share * rank)
        v_hi, v_lo = split(ins[delta][...])
        hi[pl.ds(at, share * rank), :] = v_hi
        lo[pl.ds(at, share * rank), :] = v_lo
    for level in range(row_ref.shape[0]):
        level_step(level, lambda j: row_ref[level, j], hi, lo, rank)
    out_rows = box * leaf // n_tile
    unit = min(out_rows, leaf)
    bits = n_tile.bit_length() - 1
    half = n_tile // 2
    for slot in reversed(range(n_tile)):
        relative = int(format(slot, f"0{bits}b")[::-1], 2)
        block = tile ^ relative
        for piece in range(out_rows // unit):
            n = (block * out_rows + piece * unit) // leaf
            at = pl.multiple_of(n * rank, rank)
            v_hi, v_lo = rows_of(hi, at, rank), rows_of(lo, at, rank)
            out = dot(exp_ref[n], jnp.concatenate([v_hi, v_hi, v_lo], axis=0), ((0,), (0,)))
            if unit < leaf:
                which = block % (leaf // unit)
                rows = out[:unit]
                for k in range(1, leaf // unit):
                    rows = jnp.where(which == k, out[k * unit:(k + 1) * unit], rows)
                out = rows
            target = send_ref if slot >= half else keep_ref
            at = (slot % half) * out_rows + piece * unit
            target[at:at + unit, :] = out


def tie(x, *others):
    return lax.optimization_barrier((x, *others))[0]


def shards(n_tile, n_seg, right_sides, leaf_proj, col_levels, middle_factor, row_levels, leaf_expand):
    proj, col, mid, row = leaf_proj[0], col_levels[0], middle_factor[0], row_levels[0]
    expand = jnp.swapaxes(leaf_expand[0], 1, 2)
    box, rank, leaf = proj.shape
    levels, pairs = col.shape[:2]
    chunks = right_sides.shape[1] // CHUNK
    out_rows = box * leaf // n_tile
    bits = n_tile.bit_length() - 1
    part = jax.ShapeDtypeStruct((box * rank // n_seg, CHUNK), F32)
    half = jax.ShapeDtypeStruct((box * leaf // 2, CHUNK), F32)
    params = pltpu.CompilerParams(vmem_limit_bytes=16 * 2**20)
    greedy = pltpu.CompilerParams(vmem_limit_bytes=53 * 2**20)
    cost = pl.CostEstimate(flops=600_000_000, bytes_accessed=5_000_000, transcendentals=0)
    in_hbm = pl.BlockSpec(memory_space=pltpu.HBM)
    in_vmem = pl.BlockSpec(memory_space=pltpu.VMEM)
    anywhere = pl.BlockSpec(memory_space=pl.ANY)

    def column_side(start, count):
        width = count * CHUNK
        outs = pl.pallas_call(
            functools.partial(column_kernel, n_seg, start * CHUNK),
            in_specs=[in_hbm] * 4,
            out_specs=[in_vmem] * (n_seg * count),
            out_shape=[part] * (n_seg * count),
            scratch_shapes=[
                pltpu.VMEM((box * leaf, width), F32),
                pltpu.VMEM(proj.shape, F32),
                pltpu.VMEM(col.shape, F32),
                pltpu.VMEM(mid.shape, F32),
                pltpu.VMEM((box * rank, width), BF16),
                pltpu.VMEM((box * rank, width), BF16),
                pltpu.SemaphoreType.DMA((6 + levels,)),
            ],
            compiler_params=greedy,
            cost_estimate=cost,
            name="column_side",
        )(right_sides, proj, col, mid)
        return [outs[k * n_seg:(k + 1) * n_seg] for k in range(count)]

    def row_weights(after):
        return pl.pallas_call(
            weights_kernel,
            in_specs=[anywhere, in_vmem, in_vmem],
            out_specs=[in_vmem] * 2,
            out_shape=[
                jax.ShapeDtypeStruct((levels, pairs, 2 * rank, 4 * rank), BF16),
                jax.ShapeDtypeStruct((box, 3 * rank, leaf), BF16),
            ],
            compiler_params=params,
            cost_estimate=cost,
            name="row_weights",
        )(after, row, expand)

    def row_side(parts, weights):
        return pl.pallas_call(
            functools.partial(row_kernel, n_seg, n_tile, leaf),
            in_specs=[in_vmem] * (n_seg + 2),
            out_specs=[in_vmem] * 2,
            out_shape=[half] * 2,
            scratch_shapes=[pltpu.VMEM((box * rank, CHUNK), BF16)] * 2,
            compiler_params=params,
            cost_estimate=cost,
            name="row_side",
        )(*parts, *weights)

    def swap(x, axis, size, mask):
        return lax.ppermute(x, axis, [(i, i ^ mask) for i in range(size)])

    def exchange(parts, *after):
        return [parts[0]] + [swap(tie(parts[k], *after) if after else parts[k], "seg", n_seg, k) for k in range(1, n_seg)]

    def total(terms, low, high):
        return functools.reduce(jnp.add, [x[low:high] for x in terms])

    def next_send(terms):
        left = terms[-1].shape[0]
        return total(terms, left // 2, left)

    parts = column_side(0, 1)
    received = {0: exchange(parts[0])}
    if chunks > 1:
        parts += column_side(1, chunks - 1)
        received[1] = exchange(parts[1])
    weights = row_weights(parts[-1][0])

    terms, sends = [], {}
    for c in range(chunks):
        after = [sends[c - 2, 2]] if c >= 2 else []
        arrived = [tie(x, *after) if after else x for x in received[c]]
        send, keep = row_side(arrived, weights)
        terms.append([keep, swap(send, "tile", n_tile, 1)])
        sends[c, 1] = next_send(terms[c])
        terms[c].append(swap(sends[c, 1], "tile", n_tile, 2))
        if c + 2 < chunks:
            received[c + 2] = exchange(parts[c + 2], sends[c, 1])
        if c >= 1:
            sends[c - 1, 2] = tie(next_send(terms[c - 1]), sends[c, 1])
            terms[c - 1].append(swap(sends[c - 1, 2], "tile", n_tile, 4))
    last = chunks - 1
    sends[last, 2] = next_send(terms[last])
    terms[last].append(swap(sends[last, 2], "tile", n_tile, 4))
    for c in range(chunks):
        for b in range(3, bits):
            sends[c, b] = next_send(terms[c])
            if c < last:
                sends[c, b] = tie(sends[c, b], sends[last, 1])
            terms[c].append(swap(sends[c, b], "tile", n_tile, 1 << b))
    return jnp.concatenate([total(t, 0, out_rows) for t in terms], axis=1)


def solution(mesh):
    in_specs = (
        P(("tile", "seg"), None),
        P("tile", "seg", None, None),
        P("tile", None, "seg", None, None),
        P("tile", "seg", None, None),
        P("tile", None, "seg", None, None),
        P("tile", "seg", None, None),
    )
    out_specs = P(("seg", "tile"), None)
    body = functools.partial(shards, mesh.shape["tile"], mesh.shape["seg"])
    return jax.shard_map(body, mesh=mesh, in_specs=in_specs, out_specs=out_specs, check_vma=False)
```

time: 81.4 us -> 75.6 us (0.929)
  waiting for transfers between devices: 35.3 us -> 30 us
  local copies, waits for them, and re-layouts: 5.87 us -> 0.97 us
  Pallas kernels: 13.8 us -> 17.7 us
    ppermute x20, waiting for transfers between devices: 35.3 us -> 30 us  [swap(): return lax.ppermute(x, axis, [(i, i ^ mask) for i in range(size)])]
    unnamed x14 -> x10, local copies, waits for them, and re-layouts: 5.87 us -> 0.97 us
    pallas_call x8 -> x7, Pallas kernels: 13.8 us -> 17.7 us  [the longest x2 10.8 us: column_side(): pl.pallas_call(functools.partial(column_kernel, n_seg, start * CHUNK), in...]
  transfers between devices with their start and end apart: 20 -> 20, of which waited for: 10 -> 10; matrix products, arithmetic and copies ran while one was open for 0% -> 1% of each run, Pallas kernels for 15% -> 16%
where the time goes in v2:
time: 75.6 us; the launch traced here: 75.5 us
  waiting for transfers between devices  30 us (40%)
  starting transfers between devices  25.3 us (33%)
  Pallas kernels  17.7 us (23%)
  other arithmetic  1.26 us (2%)
  local copies, waits for them, and re-layouts  0.97 us (1%)
    ppermute x20, waiting for transfers between devices, swap(): return lax.ppermute(x, axis, [(i, i ^ mask) for i in range(size)])  30 us
    ppermute x20, starting transfers between devices, swap(): return lax.ppermute(x, axis, [(i, i ^ mask) for i in range(size)])  25.3 us
    pallas_call x2, Pallas kernels, column_side(): pl.pallas_call(functools.partial(column_kernel, n_seg, start * CHUNK), in...  10.8 us
    pallas_call x4, Pallas kernels, row_side(): pl.pallas_call(functools.partial(row_kernel, n_seg, n_tile, leaf), in_spe...  6.57 us
  transfers between devices with their start and end apart: 20, of which 10 were waited for; matrix products, arithmetic and copies ran while one was open for 1% of the time, Pallas kernels for 16%

profile of v2, /device:TPU:0, one launch (start us, length us, event | category | flops | bytes accessed | tf_op | source)
XLA Modules:
  0.0 75.5 jit_solution(13313098192917875308)
XLA Ops:
  0.0 4.0 %column_side.2 = (f32[512,128]{1,0:T(8,128)S(1)}, f32[512,128]{1,0:T(8,128)S(1)}) custom-call(f32[2048,512]{1,0:T(8,128)} %x_hbm.3, f32[16,64,128]{2,1,0:T(8,128)} %bitcast.11, f32[4,8,128,128]{3,2,1,0:T(8,128)} %bitcast.9, f32[16,64,64]{2,1,0:T(8,128)} %bitcast.13), custom_call_target="tpu_custom_call" | custom-call | flops 600000000 | bytes 5000000 | tf_op jit(solution)/shard_map/column_side/pallas_call | solution.py:169
  4.0 0.0 copy-start
  4.0 0.0 copy-start.2
  4.0 3.0 %collective-permute-start = (f32[512,128]{1,0:T(8,128)S(1)}, f32[512,128]{1,0:T(8,128)S(1)}, u32[]{:S(2)}, u32[]{:S(2)}) collective-permute-start(f32[512,128]{1,0:T(8,128)S(1)} %get-tuple-element.36), channel_id=1, source_target_pairs={{0,1},{1,0},{2,3},{3,2},{4,5},{5,4},{6,7},{7,6},{8,9},{9,8},{10,11... | collective-permute-start | bytes 786440 | tf_op jit(solution)/shard_map/ppermute | solution.py:216
  7.0 6.9 %column_side.3 = (f32[512,128]{1,0:T(8,128)S(1)}, f32[512,128]{1,0:T(8,128)S(1)}, f32[512,128]{1,0:T(8,128)S(1)}, f32[512,128]{1,0:T(8,128)}, f32[512,128]{1,0:T(8,128)}, /*index=5*/f32[512,128]{1,0:T(8,128)}) custom-call(f32[2048,512]{1,0:T(8,128)} %x_hbm.3, f32[16,64,128]{2,1,0:T(8,128)} %bitcast.12, f32[4,8,128,128]{3,2,1,0:T(8,128)} %bitcast.10, ...), custom_call_target="tpu_custom_call" | custom-call | flops 600000000 | bytes 5000000 | tf_op jit(solution)/shard_map/column_side/pallas_call | solution.py:169
  13.9 0.2 collective-permute-start.3
  14.1 0.0 copy-done
  14.1 0.0 copy-done.2
  14.1 0.0 copy-start.1
  14.1 0.9 %copy-done.1 = f32[512,128]{1,0:T(8,128)S(1)} copy-done((f32[512,128]{1,0:T(8,128)S(1)}, f32[512,128]{1,0:T(8,128)}, u32[]{:S(2)}) %copy-start.1) | copy-done | bytes 262168
  15.1 0.3 row_weights.1
  15.4 0.0 collective-permute-done.refs_1_
  15.4 1.6 %row_side.4 = (f32[1024,128]{1,0:T(8,128)S(1)}, f32[1024,128]{1,0:T(8,128)S(1)}) custom-call(f32[512,128]{1,0:T(8,128)S(1)} %get-tuple-element.35.refs_0_, f32[512,128]{1,0:T(8,128)S(1)} %collective-permute-done.refs_1_, bf16[4,8,128,256]{3,2,1,0:T(8,128)(2,1)S(1)} %get-tuple-element.38.refs_2_, bf16[16,192,128]{2,1,0:T(8,128)(2,1)S(1)} %get-tuple-element.39.refs_3_), custom_call_target="tpu_custom_call" | custom-call | flops 600000000 | bytes 5000000 | tf_op jit(solution)/shard_map/row_side/pallas_call | solution.py:204
  17.0 0.1 collective-permute-start.1
  17.1 4.6 %collective-permute-done.3.refs_1_ = f32[512,128]{1,0:T(8,128)S(1)} collective-permute-done((f32[512,128]{1,0:T(8,128)S(1)}, f32[512,128]{1,0:T(8,128)S(1)}, u32[]{:S(2)}, u32[]{:S(2)}) %collective-permute-start.3) | collective-permute-done | bytes 262176 | tf_op jit(solution)/shard_map/ppermute | solution.py:216
  21.7 0.0 copy-start.4
  21.7 1.6 %row_side.5 = (f32[1024,128]{1,0:T(8,128)S(1)}, f32[1024,128]{1,0:T(8,128)S(1)}) custom-call(f32[512,128]{1,0:T(8,128)S(1)} %get-tuple-element.42.refs_0_, f32[512,128]{1,0:T(8,128)S(1)} %collective-permute-done.3.refs_1_, bf16[4,8,128,256]{3,2,1,0:T(8,128)(2,1)S(1)} %get-tuple-element.38.refs_2_, bf16[16,192,128]{2,1,0:T(8,128)(2,1)S(1)} %get-tuple-element.39.refs_3_), custom_call_target="tpu_custom_call" | custom-call | flops 600000000 | bytes 5000000 | tf_op jit(solution)/shard_map/row_side/pallas_call | solution.py:204
  23.4 0.1 collective-permute-start.4
  23.4 0.0 collective-permute-done.1
  23.5 1.6 %collective-permute-start.2 = (f32[512,128]{1,0:T(8,128)S(1)}, f32[512,128]{1,0:T(8,128)S(1)}, u32[]{:S(2)}, u32[]{:S(2)}) collective-permute-start(f32[512,128]{1,0:T(8,128)S(1)} %slice_add_fusion.3), channel_id=1, source_target_pairs={{0,4},{2,6},{4,0},{6,2},{8,12},{10,14},{12,8},{14,10},{16,20},{18,... | collective-permute-start | bytes 786440 | tf_op jit(solution)/shard_map/ppermute | solution.py:216
  25.1 0.0 copy-done.4
  25.1 0.7 collective-permute-start.7
  25.8 0.0 collective-permute-done.4
  25.8 0.0 copy-start.3
  25.8 6.4 %collective-permute-done.2 = f32[512,128]{1,0:T(8,128)S(1)} collective-permute-done((f32[512,128]{1,0:T(8,128)S(1)}, f32[512,128]{1,0:T(8,128)S(1)}, u32[]{:S(2)}, u32[]{:S(2)}) %collective-permute-start.2) | collective-permute-done | bytes 262176 | tf_op jit(solution)/shard_map/ppermute | solution.py:216
  32.3 1.2 %collective-permute-done.7.refs_1_ = f32[512,128]{1,0:T(8,128)S(1)} collective-permute-done((f32[512,128]{1,0:T(8,128)S(1)}, f32[512,128]{1,0:T(8,128)S(1)}, u32[]{:S(2)}, u32[]{:S(2)}) %collective-permute-start.7) | collective-permute-done | bytes 262176 | tf_op jit(solution)/shard_map/ppermute | solution.py:216
  33.5 1.6 %row_side.6 = (f32[1024,128]{1,0:T(8,128)S(1)}, f32[1024,128]{1,0:T(8,128)S(1)}) custom-call(f32[512,128]{1,0:T(8,128)S(1)} %get-tuple-element.48.refs_0_, f32[512,128]{1,0:T(8,128)S(1)} %collective-permute-done.7.refs_1_, bf16[4,8,128,256]{3,2,1,0:T(8,128)(2,1)S(1)} %get-tuple-element.38.refs_2_, bf16[16,192,128]{2,1,0:T(8,128)(2,1)S(1)} %get-tuple-element.39.refs_3_), custom_call_target="tpu_custom_call" | custom-call | flops 600000000 | bytes 5000000 | tf_op jit(solution)/shard_map/row_side/pallas_call | solution.py:204
  35.1 0.1 collective-permute-start.8
  35.2 0.6 collective-permute-start.6
  35.8 0.0 copy-done.3
  35.8 0.6 collective-permute-start.9
  36.4 1.7 %collective-permute-start.5 = (f32[256,128]{1,0:T(8,128)S(1)}, f32[256,128]{1,0:T(8,128)S(1)}, u32[]{:S(2)}, u32[]{:S(2)}) collective-permute-start(f32[256,128]{1,0:T(8,128)S(1)} %slice_add_fusion.10), channel_id=1, source_target_pairs={{0,8},{2,10},{4,12},{6,14},{8,0},{10,2},{12,4},{14,6},{16,24},{18,... | collective-permute-start | bytes 393224 | tf_op jit(solution)/shard_map/ppermute | solution.py:216
  38.1 5.9 %collective-permute-done.6 = f32[512,128]{1,0:T(8,128)S(1)} collective-permute-done((f32[512,128]{1,0:T(8,128)S(1)}, f32[512,128]{1,0:T(8,128)S(1)}, u32[]{:S(2)}, u32[]{:S(2)}) %collective-permute-start.6) | collective-permute-done | bytes 262176 | tf_op jit(solution)/shard_map/ppermute | solution.py:216
  44.0 0.0 collective-permute-done.8
  44.0 0.2 slice_add_fusion.1
  44.2 0.0 collective-permute-done.9.refs_1_
  44.2 1.6 %row_side.7 = (f32[1024,128]{1,0:T(8,128)S(1)}, f32[1024,128]{1,0:T(8,128)S(1)}) custom-call(f32[512,128]{1,0:T(8,128)S(1)} %copy-done.1, f32[512,128]{1,0:T(8,128)S(1)} %collective-permute-done.9.refs_1_, bf16[4,8,128,256]{3,2,1,0:T(8,128)(2,1)S(1)} %get-tuple-element.38.refs_2_, bf16[16,192,128]{2,1,0:T(8,128)(2,1)S(1)} %get-tuple-element.39.refs_3_), custom_call_target="tpu_custom_call" | custom-call | flops 600000000 | bytes 5000000 | tf_op jit(solution)/shard_map/row_side/pallas_call | solution.py:204
  45.9 0.1 collective-permute-start.10
  45.9 1.6 %collective-permute-start.12 = (f32[256,128]{1,0:T(8,128)S(1)}, f32[256,128]{1,0:T(8,128)S(1)}, u32[]{:S(2)}, u32[]{:S(2)}) collective-permute-start(f32[256,128]{1,0:T(8,128)S(1)} %slice_add_fusion.8), channel_id=1, source_target_pairs={{0,8},{2,10},{4,12},{6,14},{8,0},{10,2},{12,4},{14,6},{16,24},{18,... | collective-permute-start | bytes 393224 | tf_op jit(solution)/shard_map/ppermute | solution.py:216
  47.6 0.0 collective-permute-done.5
  47.6 1.5 %collective-permute-start.14 = (f32[512,128]{1,0:T(8,128)S(1)}, f32[512,128]{1,0:T(8,128)S(1)}, u32[]{:S(2)}, u32[]{:S(2)}) collective-permute-start(f32[512,128]{1,0:T(8,128)S(1)} %slice_add_fusion.1), channel_id=1, source_target_pairs={{0,4},{2,6},{4,0},{6,2},{8,12},{10,14},{12,8},{14,10},{16,20},{18,... | collective-permute-start | bytes 786440 | tf_op jit(solution)/shard_map/ppermute | solution.py:216
  49.1 2.7 %collective-permute-done.12 = f32[256,128]{1,0:T(8,128)S(1)} collective-permute-done((f32[256,128]{1,0:T(8,128)S(1)}, f32[256,128]{1,0:T(8,128)S(1)}, u32[]{:S(2)}, u32[]{:S(2)}) %collective-permute-start.12) | collective-permute-done | bytes 131104 | tf_op jit(solution)/shard_map/ppermute | solution.py:216
  51.9 0.0 collective-permute-done.10
  51.9 2.7 %collective-permute-start.13 = (f32[128,128]{1,0:T(8,128)S(1)}, f32[128,128]{1,0:T(8,128)S(1)}, u32[]{:S(2)}, u32[]{:S(2)}) collective-permute-start(f32[128,128]{1,0:T(8,128)S(1)} %slice_add_fusion.24), channel_id=1, source_target_pairs={{0,16},{2,18},{4,20},{6,22},{8,24},{10,26},{12,28},{14,30},{16,0},... | collective-permute-start | bytes 196616 | tf_op jit(solution)/shard_map/ppermute | solution.py:216
  54.6 1.5 %collective-permute-done.14 = f32[512,128]{1,0:T(8,128)S(1)} collective-permute-done((f32[512,128]{1,0:T(8,128)S(1)}, f32[512,128]{1,0:T(8,128)S(1)}, u32[]{:S(2)}, u32[]{:S(2)}) %collective-permute-start.14) | collective-permute-done | bytes 262176 | tf_op jit(solution)/shard_map/ppermute | solution.py:216
  56.1 1.5 %collective-permute-start.17 = (f32[512,128]{1,0:T(8,128)S(1)}, f32[512,128]{1,0:T(8,128)S(1)}, u32[]{:S(2)}, u32[]{:S(2)}) collective-permute-start(f32[512,128]{1,0:T(8,128)S(1)} %slice_add_fusion), channel_id=1, source_target_pairs={{0,4},{2,6},{4,0},{6,2},{8,12},{10,14},{12,8},{14,10},{16,20},{18,... | collective-permute-start | bytes 786440 | tf_op jit(solution)/shard_map/ppermute | solution.py:216
  57.6 0.4 collective-permute-start.15
  58.1 2.6 %collective-permute-start.11 = (f32[128,128]{1,0:T(8,128)S(1)}, f32[128,128]{1,0:T(8,128)S(1)}, u32[]{:S(2)}, u32[]{:S(2)}) collective-permute-start(f32[128,128]{1,0:T(8,128)S(1)} %slice_add_fusion.30), channel_id=1, source_target_pairs={{0,16},{2,18},{4,20},{6,22},{8,24},{10,26},{12,28},{14,30},{16,0},... | collective-permute-start | bytes 196616 | tf_op jit(solution)/shard_map/ppermute | solution.py:216
  60.7 0.0 collective-permute-done.13
  60.7 3.2 %collective-permute-done.11 = f32[128,128]{1,0:T(8,128)S(1)} collective-permute-done((f32[128,128]{1,0:T(8,128)S(1)}, f32[128,128]{1,0:T(8,128)S(1)}, u32[]{:S(2)}, u32[]{:S(2)}) %collective-permute-start.11) | collective-permute-done | bytes 65568 | tf_op jit(solution)/shard_map/ppermute | solution.py:216
  64.0 0.0 collective-permute-done.17
  64.0 2.2 %collective-permute-start.18 = (f32[256,128]{1,0:T(8,128)S(1)}, f32[256,128]{1,0:T(8,128)S(1)}, u32[]{:S(2)}, u32[]{:S(2)}) collective-permute-start(f32[256,128]{1,0:T(8,128)S(1)} %slice_add_fusion.4), channel_id=1, source_target_pairs={{0,8},{2,10},{4,12},{6,14},{8,0},{10,2},{12,4},{14,6},{16,24},{18,... | collective-permute-start | bytes 393224 | tf_op jit(solution)/shard_map/ppermute | solution.py:216
  66.2 0.0 collective-permute-done.15
  66.2 2.0 %collective-permute-start.16 = (f32[128,128]{1,0:T(8,128)S(1)}, f32[128,128]{1,0:T(8,128)S(1)}, u32[]{:S(2)}, u32[]{:S(2)}) collective-permute-start(f32[128,128]{1,0:T(8,128)S(1)} %slice_add_fusion.18), channel_id=1, source_target_pairs={{0,16},{2,18},{4,20},{6,22},{8,24},{10,26},{12,28},{14,30},{16,0},... | collective-permute-start | bytes 196616 | tf_op jit(solution)/shard_map/ppermute | solution.py:216
  68.2 1.2 %collective-permute-done.18 = f32[256,128]{1,0:T(8,128)S(1)} collective-permute-done((f32[256,128]{1,0:T(8,128)S(1)}, f32[256,128]{1,0:T(8,128)S(1)}, u32[]{:S(2)}, u32[]{:S(2)}) %collective-permute-start.18) | collective-permute-done | bytes 131104 | tf_op jit(solution)/shard_map/ppermute | solution.py:216
  69.5 1.9 %collective-permute-start.19 = (f32[128,128]{1,0:T(8,128)S(1)}, f32[128,128]{1,0:T(8,128)S(1)}, u32[]{:S(2)}, u32[]{:S(2)}) collective-permute-start(f32[128,128]{1,0:T(8,128)S(1)} %slice_add_fusion.12), channel_id=1, source_target_pairs={{0,16},{2,18},{4,20},{6,22},{8,24},{10,26},{12,28},{14,30},{16,0},... | collective-permute-start | bytes 196616 | tf_op jit(solution)/shard_map/ppermute | solution.py:216
  71.4 1.4 %collective-permute-done.16 = f32[128,128]{1,0:T(8,128)S(1)} collective-permute-done((f32[128,128]{1,0:T(8,128)S(1)}, f32[128,128]{1,0:T(8,128)S(1)}, u32[]{:S(2)}, u32[]{:S(2)}) %collective-permute-start.16) | collective-permute-done | bytes 65568 | tf_op jit(solution)/shard_map/ppermute | solution.py:216
  72.9 1.8 %collective-permute-done.19 = f32[128,128]{1,0:T(8,128)S(1)} collective-permute-done((f32[128,128]{1,0:T(8,128)S(1)}, f32[128,128]{1,0:T(8,128)S(1)}, u32[]{:S(2)}, u32[]{:S(2)}) %collective-permute-start.19) | collective-permute-done | bytes 65568 | tf_op jit(solution)/shard_map/ppermute | solution.py:216
  74.7 0.7 pad_maximum_fusion
  (15 shorter events, 0.3 us)
Async XLA Ops:
  4.0 10.2 %copy-start = (f32[1,4,8,128,128]{4,3,2,1,0:T(8,128)S(1)}, f32[1,4,8,128,128]{4,3,2,1,0:T(8,128)}, u32[]{:S(2)}) copy-start(f32[1,4,8,128,128]{4,3,2,1,0:T(8,128)} %param.10) | copy-start | bytes 6291460
  4.0 10.1 %copy-start.2 = (f32[1,16,128,64]{2,3,1,0:T(8,128)S(1)}, f32[1,16,128,64]{2,3,1,0:T(8,128)}, u32[]{:S(2)}) copy-start(f32[1,16,128,64]{2,3,1,0:T(8,128)} %param.11) | copy-start | bytes 1572868
  4.0 11.4 %collective-permute-start = (f32[512,128]{1,0:T(8,128)S(1)}, f32[512,128]{1,0:T(8,128)S(1)}, u32[]{:S(2)}, u32[]{:S(2)}) collective-permute-start(f32[512,128]{1,0:T(8,128)S(1)} %get-tuple-element.36), channel_id=1, source_target_pairs={{0,1},{1,0},{2,3},{3,2},{4,5},{5,4},{6,7},{7,6},{8,9},{9,8},{10,11... | collective-permute-start | bytes 786440 | tf_op jit(solution)/shard_map/ppermute | solution.py:216
  13.9 7.8 %collective-permute-start.3 = (f32[512,128]{1,0:T(8,128)S(1)}, f32[512,128]{1,0:T(8,128)S(1)}, u32[]{:S(2)}, u32[]{:S(2)}) collective-permute-start(f32[512,128]{1,0:T(8,128)S(1)} %get-tuple-element.43), channel_id=1, source_target_pairs={{0,1},{1,0},{2,3},{3,2},{4,5},{5,4},{6,7},{7,6},{8,9},{9,8},{10,11... | collective-permute-start | bytes 786440 | tf_op jit(solution)/shard_map/ppermute | solution.py:216
  14.1 1.0 %copy-start.1 = (f32[512,128]{1,0:T(8,128)S(1)}, f32[512,128]{1,0:T(8,128)}, u32[]{:S(2)}) copy-start(f32[512,128]{1,0:T(8,128)} %get-tuple-element.55.after_ref.refs_0_) | copy-start | bytes 786436
  17.0 6.4 %collective-permute-start.1 = (f32[1024,128]{1,0:T(8,128)S(1)}, f32[1024,128]{1,0:T(8,128)S(1)}, u32[]{:S(2)}, u32[]{:S(2)}) collective-permute-start(f32[1024,128]{1,0:T(8,128)S(1)} %get-tuple-element.41), channel_id=1, source_target_pairs={{0,2},{2,0},{4,6},{6,4},{8,10},{10,8},{12,14},{14,12},{16,18},{18,... | collective-permute-start | bytes 1572872 | tf_op jit(solution)/shard_map/ppermute | solution.py:216
  21.7 3.4 %copy-start.4 = (f32[512,128]{1,0:T(8,128)S(1)}, f32[512,128]{1,0:T(8,128)}, u32[]{:S(2)}) copy-start(f32[512,128]{1,0:T(8,128)} %get-tuple-element.50) | copy-start | bytes 786436
  23.4 2.4 %collective-permute-start.4 = (f32[1024,128]{1,0:T(8,128)S(1)}, f32[1024,128]{1,0:T(8,128)S(1)}, u32[]{:S(2)}, u32[]{:S(2)}) collective-permute-start(f32[1024,128]{1,0:T(8,128)S(1)} %get-tuple-element.45), channel_id=1, source_target_pairs={{0,2},{2,0},{4,6},{6,4},{8,10},{10,8},{12,14},{14,12},{16,18},{18,... | collective-permute-start | bytes 1572872 | tf_op jit(solution)/shard_map/ppermute | solution.py:216
  23.5 8.8 %collective-permute-start.2 = (f32[512,128]{1,0:T(8,128)S(1)}, f32[512,128]{1,0:T(8,128)S(1)}, u32[]{:S(2)}, u32[]{:S(2)}) collective-permute-start(f32[512,128]{1,0:T(8,128)S(1)} %slice_add_fusion.3), channel_id=1, source_target_pairs={{0,4},{2,6},{4,0},{6,2},{8,12},{10,14},{12,8},{14,10},{16,20},{18,... | collective-permute-start | bytes 786440 | tf_op jit(solution)/shard_map/ppermute | solution.py:216
  25.1 8.4 %collective-permute-start.7 = (f32[512,128]{1,0:T(8,128)S(1)}, f32[512,128]{1,0:T(8,128)S(1)}, u32[]{:S(2)}, u32[]{:S(2)}) collective-permute-start(f32[512,128]{1,0:T(8,128)S(1)} %copy-done.4), channel_id=1, source_target_pairs={{0,1},{1,0},{2,3},{3,2},{4,5},{5,4},{6,7},{7,6},{8,9},{9,8},{10,11... | collective-permute-start | bytes 786440 | tf_op jit(solution)/shard_map/ppermute | solution.py:216
  25.8 10.0 %copy-start.3 = (f32[512,128]{1,0:T(8,128)S(1)}, f32[512,128]{1,0:T(8,128)}, u32[]{:S(2)}) copy-start(f32[512,128]{1,0:T(8,128)} %get-tuple-element.57) | copy-start | bytes 786436
  35.1 8.8 %collective-permute-start.8 = (f32[1024,128]{1,0:T(8,128)S(1)}, f32[1024,128]{1,0:T(8,128)S(1)}, u32[]{:S(2)}, u32[]{:S(2)}) collective-permute-start(f32[1024,128]{1,0:T(8,128)S(1)} %get-tuple-element.53), channel_id=1, source_target_pairs={{0,2},{2,0},{4,6},{6,4},{8,10},{10,8},{12,14},{14,12},{16,18},{18,... | collective-permute-start | bytes 1572872 | tf_op jit(solution)/shard_map/ppermute | solution.py:216
  35.2 8.7 %collective-permute-start.6 = (f32[512,128]{1,0:T(8,128)S(1)}, f32[512,128]{1,0:T(8,128)S(1)}, u32[]{:S(2)}, u32[]{:S(2)}) collective-permute-start(f32[512,128]{1,0:T(8,128)S(1)} %slice_add_fusion.2), channel_id=1, source_target_pairs={{0,4},{2,6},{4,0},{6,2},{8,12},{10,14},{12,8},{14,10},{16,20},{18,... | collective-permute-start | bytes 786440 | tf_op jit(solution)/shard_map/ppermute | solution.py:216
  35.8 8.4 %collective-permute-start.9 = (f32[512,128]{1,0:T(8,128)S(1)}, f32[512,128]{1,0:T(8,128)S(1)}, u32[]{:S(2)}, u32[]{:S(2)}) collective-permute-start(f32[512,128]{1,0:T(8,128)S(1)} %copy-done.3), channel_id=1, source_target_pairs={{0,1},{1,0},{2,3},{3,2},{4,5},{5,4},{6,7},{7,6},{8,9},{9,8},{10,11... | collective-permute-start | bytes 786440 | tf_op jit(solution)/shard_map/ppermute | solution.py:216
  36.4 11.2 %collective-permute-start.5 = (f32[256,128]{1,0:T(8,128)S(1)}, f32[256,128]{1,0:T(8,128)S(1)}, u32[]{:S(2)}, u32[]{:S(2)}) collective-permute-start(f32[256,128]{1,0:T(8,128)S(1)} %slice_add_fusion.10), channel_id=1, source_target_pairs={{0,8},{2,10},{4,12},{6,14},{8,0},{10,2},{12,4},{14,6},{16,24},{18,... | collective-permute-start | bytes 393224 | tf_op jit(solution)/shard_map/ppermute | solution.py:216
  45.9 6.0 %collective-permute-start.10 = (f32[1024,128]{1,0:T(8,128)S(1)}, f32[1024,128]{1,0:T(8,128)S(1)}, u32[]{:S(2)}, u32[]{:S(2)}) collective-permute-start(f32[1024,128]{1,0:T(8,128)S(1)} %get-tuple-element.60), channel_id=1, source_target_pairs={{0,2},{2,0},{4,6},{6,4},{8,10},{10,8},{12,14},{14,12},{16,18},{18,... | collective-permute-start | bytes 1572872 | tf_op jit(solution)/shard_map/ppermute | solution.py:216
  45.9 5.9 %collective-permute-start.12 = (f32[256,128]{1,0:T(8,128)S(1)}, f32[256,128]{1,0:T(8,128)S(1)}, u32[]{:S(2)}, u32[]{:S(2)}) collective-permute-start(f32[256,128]{1,0:T(8,128)S(1)} %slice_add_fusion.8), channel_id=1, source_target_pairs={{0,8},{2,10},{4,12},{6,14},{8,0},{10,2},{12,4},{14,6},{16,24},{18,... | collective-permute-start | bytes 393224 | tf_op jit(solution)/shard_map/ppermute | solution.py:216
  47.6 8.4 %collective-permute-start.14 = (f32[512,128]{1,0:T(8,128)S(1)}, f32[512,128]{1,0:T(8,128)S(1)}, u32[]{:S(2)}, u32[]{:S(2)}) collective-permute-start(f32[512,128]{1,0:T(8,128)S(1)} %slice_add_fusion.1), channel_id=1, source_target_pairs={{0,4},{2,6},{4,0},{6,2},{8,12},{10,14},{12,8},{14,10},{16,20},{18,... | collective-permute-start | bytes 786440 | tf_op jit(solution)/shard_map/ppermute | solution.py:216
  51.9 8.8 %collective-permute-start.13 = (f32[128,128]{1,0:T(8,128)S(1)}, f32[128,128]{1,0:T(8,128)S(1)}, u32[]{:S(2)}, u32[]{:S(2)}) collective-permute-start(f32[128,128]{1,0:T(8,128)S(1)} %slice_add_fusion.24), channel_id=1, source_target_pairs={{0,16},{2,18},{4,20},{6,22},{8,24},{10,26},{12,28},{14,30},{16,0},... | collective-permute-start | bytes 196616 | tf_op jit(solution)/shard_map/ppermute | solution.py:216
  56.1 7.9 %collective-permute-start.17 = (f32[512,128]{1,0:T(8,128)S(1)}, f32[512,128]{1,0:T(8,128)S(1)}, u32[]{:S(2)}, u32[]{:S(2)}) collective-permute-start(f32[512,128]{1,0:T(8,128)S(1)} %slice_add_fusion), channel_id=1, source_target_pairs={{0,4},{2,6},{4,0},{6,2},{8,12},{10,14},{12,8},{14,10},{16,20},{18,... | collective-permute-start | bytes 786440 | tf_op jit(solution)/shard_map/ppermute | solution.py:216
  57.6 8.6 %collective-permute-start.15 = (f32[256,128]{1,0:T(8,128)S(1)}, f32[256,128]{1,0:T(8,128)S(1)}, u32[]{:S(2)}, u32[]{:S(2)}) collective-permute-start(f32[256,128]{1,0:T(8,128)S(1)} %slice_add_fusion.6), channel_id=1, source_target_pairs={{0,8},{2,10},{4,12},{6,14},{8,0},{10,2},{12,4},{14,6},{16,24},{18,... | collective-permute-start | bytes 393224 | tf_op jit(solution)/shard_map/ppermute | solution.py:216
  58.1 5.9 %collective-permute-start.11 = (f32[128,128]{1,0:T(8,128)S(1)}, f32[128,128]{1,0:T(8,128)S(1)}, u32[]{:S(2)}, u32[]{:S(2)}) collective-permute-start(f32[128,128]{1,0:T(8,128)S(1)} %slice_add_fusion.30), channel_id=1, source_target_pairs={{0,16},{2,18},{4,20},{6,22},{8,24},{10,26},{12,28},{14,30},{16,0},... | collective-permute-start | bytes 196616 | tf_op jit(solution)/shard_map/ppermute | solution.py:216
  64.0 5.5 %collective-permute-start.18 = (f32[256,128]{1,0:T(8,128)S(1)}, f32[256,128]{1,0:T(8,128)S(1)}, u32[]{:S(2)}, u32[]{:S(2)}) collective-permute-start(f32[256,128]{1,0:T(8,128)S(1)} %slice_add_fusion.4), channel_id=1, source_target_pairs={{0,8},{2,10},{4,12},{6,14},{8,0},{10,2},{12,4},{14,6},{16,24},{18,... | collective-permute-start | bytes 393224 | tf_op jit(solution)/shard_map/ppermute | solution.py:216
  66.2 6.6 %collective-permute-start.16 = (f32[128,128]{1,0:T(8,128)S(1)}, f32[128,128]{1,0:T(8,128)S(1)}, u32[]{:S(2)}, u32[]{:S(2)}) collective-permute-start(f32[128,128]{1,0:T(8,128)S(1)} %slice_add_fusion.18), channel_id=1, source_target_pairs={{0,16},{2,18},{4,20},{6,22},{8,24},{10,26},{12,28},{14,30},{16,0},... | collective-permute-start | bytes 196616 | tf_op jit(solution)/shard_map/ppermute | solution.py:216
  69.5 5.2 %collective-permute-start.19 = (f32[128,128]{1,0:T(8,128)S(1)}, f32[128,128]{1,0:T(8,128)S(1)}, u32[]{:S(2)}, u32[]{:S(2)}) collective-permute-start(f32[128,128]{1,0:T(8,128)S(1)} %slice_add_fusion.12), channel_id=1, source_target_pairs={{0,16},{2,18},{4,20},{6,22},{8,24},{10,26},{12,28},{14,30},{16,0},... | collective-permute-start | bytes 196616 | tf_op jit(solution)/shard_map/ppermute | solution.py:216
